TPU v7x, 32 devices: a whole 2x2x4 slice. The times are simulated.
32 devices in a mesh: heads: 2 (over y), seq: 16 (over z, x, core).
Axes of the slice: x: 2, y: 2, z: 4, core: 2. Of those that a mesh axis runs over, the one named last changes fastest.
Arguments:
- inputs: bfloat16 [2, 16, 256, 1024], P(None, 'seq', 'heads'), may hold values from -6 to 6
- cotangent: bfloat16 [2, 16, 256, 1024], P(None, 'seq', 'heads'), may hold values from -6 to 6
- attn_gain: float32 [1024], replicated, may hold values from 0.25 to 1.75
- w_query: bfloat16 [1024, 1024], P(('heads', 'seq')), may hold values from -0.1875 to 0.1875
- w_key: bfloat16 [1024, 512], P(('heads', 'seq')), may hold values from -0.1875 to 0.1875
- w_value: bfloat16 [1024, 512], P(('heads', 'seq')), may hold values from -0.1875 to 0.1875
- w_output: bfloat16 [1024, 1024], P(('heads', 'seq')), may hold values from -1 to 1
- query_gain: float32 [64], replicated, may hold values from 0.25 to 1.75
- key_gain: float32 [64], replicated, may hold values from 0.25 to 1.75
- ffn_gain: float32 [1024], replicated, may hold values from 0.25 to 1.75
- w_gate: bfloat16 [1024, 4608], P(('heads', 'seq')), may hold values from -0.1875 to 0.1875
- w_up: bfloat16 [1024, 4608], P(('heads', 'seq')), may hold values from -0.1875 to 0.1875
- w_down: bfloat16 [4608, 1024], P(('heads', 'seq')), may hold values from -0.09375 to 0.09375
- doc_starts: int32 [2, 3], replicated, may hold values from 0 to 3072, as said below
Outputs:
- block_out: bfloat16 [2, 16, 256, 1024], P(None, 'seq', 'heads')
- grad_inputs: float32 [2, 16, 256, 1024], P(None, 'seq', 'heads')
- grad_attn_gain: float32 [1024], replicated
- grad_w_query: float32 [1024, 1024], P(('heads', 'seq'))
- grad_w_key: float32 [1024, 512], P(('heads', 'seq'))
- grad_w_value: float32 [1024, 512], P(('heads', 'seq'))
- grad_w_output: float32 [1024, 1024], P(('heads', 'seq'))
- grad_query_gain: float32 [64], replicated
- grad_key_gain: float32 [64], replicated
- grad_ffn_gain: float32 [1024], replicated
- grad_w_gate: float32 [1024, 4608], P(('heads', 'seq'))
- grad_w_up: float32 [1024, 4608], P(('heads', 'seq'))
- grad_w_down: float32 [4608, 1024], P(('heads', 'seq'))
Inputs may be any that keep to these rules, and one draw needn't show every extreme that they name: `doc_starts`: each row holds the 3 document starts of one micro-batch, ascending, multiples of 1024, the first 0. In one micro-batch, drawn from the seed, all are 0 (one document spans the whole sequence); in every other one they are distinct and the last is the largest value allowed.
All inputs are finite; a program needn't handle non-finite values.
Results may differ from a plain program's by a relative error of at most 0.023.
Values may be sent and summed in bfloat16 or wider, within the bound.
No kernel may reach another device: no remote copies, remote signals or barrier semaphores. Data moves between devices by JAX's collectives and lax.ppermute only.
A program may use at most 192 MiB of HBM per device.

v0:
```python
import jax
import jax.numpy as jnp
from jax import lax
from jax.sharding import PartitionSpec as P

EPS = 1e-05
THETA = 1000000.0
NEG = -1e30


def as_sent(shard):

    def short(part):
        return part.astype(jnp.bfloat16) if part.dtype == jnp.float32 else part

    return jax.tree.map(short, shard)


def rms_scale(values):
    return values * lax.rsqrt(jnp.mean(values * values, axis=-1, keepdims=True) + EPS)


def norm_back(values, gain_vec, upstream):
    inverse = lax.rsqrt(jnp.mean(values * values, axis=-1, keepdims=True) + EPS)
    scaled = upstream * gain_vec
    inner_mean = jnp.mean(scaled * values, axis=-1, keepdims=True)
    grad_values = inverse * scaled - values * inverse * inverse * inverse * inner_mean
    return (grad_values, upstream * values * inverse)


def doc_begin(starts, token_pos):
    return jnp.max(jnp.where(starts[None, :] <= token_pos[:, None], starts[None, :], 0), axis=1)


def rope_tables(positions, head_width):
    half_width = head_width // 2
    frequency = THETA ** (-(jnp.arange(half_width, dtype=jnp.float32) * 2.0 / head_width))
    angles = positions.astype(jnp.float32)[:, None] * frequency[None, :]
    return (jnp.cos(angles), jnp.sin(angles))


def rotate(values, cos_table, sin_table):
    half_width = values.shape[-1] // 2
    first_half = values[..., :half_width]
    second_half = values[..., half_width:]
    cos_rows = cos_table[:, None, :]
    sin_rows = sin_table[:, None, :]
    return jnp.concatenate(
        [
            first_half * cos_rows - second_half * sin_rows,
            second_half * cos_rows + first_half * sin_rows,
        ],
        axis=-1,
    )


def dot_plain(left_side, right_side):
    return jnp.dot(left_side, right_side, preferred_element_type=jnp.float32)


def dot_back(left_side, right_side):
    return lax.dot_general(
        left_side, right_side, (((1,), (1,)), ((), ())), preferred_element_type=jnp.float32
    )


def dot_outer(left_side, right_side):
    return lax.dot_general(
        left_side, right_side, (((0,), (0,)), ((), ())), preferred_element_type=jnp.float32
    )


def block_scores(query_here, key_block, row_pos, row_begin, first_key, starts, score_scale):
    key_width = key_block.shape[0]
    key_pos = first_key + jnp.arange(key_width, dtype=jnp.int32)
    allowed = (key_pos[None, :] <= row_pos[:, None]) & (
        doc_begin(starts, key_pos)[None, :] == row_begin[:, None]
    )
    scores = (
        jnp.einsum("qkgd,tkd->kgqt", query_here, key_block, preferred_element_type=jnp.float32)
        * score_scale
    )
    return (jnp.where(allowed, scores, NEG), allowed)


def rows_of(parts):
    return jax.tree.map(
        lambda part, own: part.astype(own.dtype),
        lax.all_gather(as_sent(parts), "heads", axis=0, tiled=True),
        parts,
    )


def part_sum(pairs):
    total = None
    for left_side, right_side, transposed in pairs:
        product = (
            dot_back(left_side, right_side) if transposed else dot_plain(left_side, right_side)
        )
        total = product if total is None else total + product
    return lax.psum_scatter(
        total.astype(jnp.bfloat16), "heads", scatter_dimension=0, tiled=True
    ).astype(jnp.float32)


def per_device(
    inputs,
    cotangent,
    attn_gain,
    w_query,
    w_key,
    w_value,
    w_output,
    query_gain,
    key_gain,
    ffn_gain,
    w_gate,
    w_up,
    w_down,
    doc_starts,
):
    head_count = lax.axis_size("heads")
    seq_index = lax.axis_index("seq")
    tok_rows = inputs.shape[2]
    block_rows = tok_rows * head_count
    total_rows = block_rows * lax.axis_size("seq")
    query_width = w_query.shape[1]
    kv_width = w_key.shape[1]
    head_size = query_gain.shape[0]
    kv_local = kv_width // head_size // head_count
    groups = query_width // kv_width
    score_scale = head_size ** (-0.5)
    shards = (w_query, w_key, w_value, w_output, w_gate, w_up, w_down)
    local_sums = None
    gain_totals = (
        jnp.zeros_like(attn_gain),
        jnp.zeros_like(query_gain),
        jnp.zeros_like(key_gain),
        jnp.zeros_like(ffn_gain),
    )
    out_list = []
    input_grads = []
    for batch_index in range(inputs.shape[0]):
        starts = doc_starts[batch_index]
        residual_in = inputs[batch_index, 0].astype(jnp.float32)
        grad_block = cotangent[batch_index, 0].astype(jnp.float32)
        cot_low = cotangent[batch_index, 0]
        row_pos = seq_index * block_rows + jnp.arange(block_rows, dtype=jnp.int32)
        row_begin = doc_begin(starts, row_pos)
        normed = (rms_scale(residual_in) * attn_gain).astype(jnp.bfloat16)
        rows_w = (
            lax.all_gather(shards[0], "seq", axis=0, tiled=True),
            lax.all_gather(shards[1], "seq", axis=0, tiled=True),
            lax.all_gather(shards[2], "seq", axis=0, tiled=True),
            lax.all_gather(shards[3], "seq", axis=0, tiled=True),
            lax.all_gather(shards[4], "seq", axis=0, tiled=True),
            lax.all_gather(shards[5], "seq", axis=0, tiled=True),
            lax.all_gather(shards[6], "seq", axis=0, tiled=True),
        )
        cols_w = (
            lax.all_to_all(rows_w[0], "heads", split_axis=1, concat_axis=0, tiled=True),
            lax.all_to_all(rows_w[1], "heads", split_axis=1, concat_axis=0, tiled=True),
            lax.all_to_all(rows_w[2], "heads", split_axis=1, concat_axis=0, tiled=True),
            lax.all_to_all(rows_w[4], "heads", split_axis=1, concat_axis=0, tiled=True),
            lax.all_to_all(rows_w[5], "heads", split_axis=1, concat_axis=0, tiled=True),
        )
        wq_use, wk_use, wv_use, wg_use, wu_use = cols_w
        wo_use = rows_w[3]
        wd_use = rows_w[6]
        normed_all, cot_all = rows_of((normed, cot_low))
        cos_table, sin_table = rope_tables(row_pos - row_begin, head_size)
        query_raw = dot_plain(normed_all, wq_use).reshape(block_rows, -1, head_size)
        key_raw = dot_plain(normed_all, wk_use).reshape(block_rows, -1, head_size)
        value_raw = dot_plain(normed_all, wv_use)
        query_rot = rotate(rms_scale(query_raw) * query_gain, cos_table, sin_table).astype(
            jnp.bfloat16
        )
        key_rot = rotate(rms_scale(key_raw) * key_gain, cos_table, sin_table).astype(jnp.bfloat16)
        query_flat = query_rot.reshape(block_rows, 1, -1)
        key_flat = key_rot.reshape(block_rows, 1, -1)
        value_flat = value_raw.astype(jnp.bfloat16).reshape(block_rows, 1, -1)
        query_here = query_flat.reshape(block_rows, kv_local, groups, head_size)
        key_all, value_all = (
            lax.all_gather(key_flat, "seq", axis=0, tiled=True),
            lax.all_gather(value_flat, "seq", axis=0, tiled=True),
        )
        key_width = 512
        key_blocks = key_all.reshape(total_rows // key_width, key_width, kv_local, head_size)
        value_blocks = value_all.reshape(total_rows // key_width, key_width, kv_local, head_size)
        firsts = key_width * jnp.arange(total_rows // key_width, dtype=jnp.int32)

        def attend_block(state_in, key_block, value_block, first_key):
            running, row_total, row_accum = state_in
            scores, allowed = block_scores(
                query_here, key_block, row_pos, row_begin, first_key, starts, score_scale
            )
            newmax = jnp.maximum(running, jnp.max(scores, axis=-1))
            exps = jnp.where(allowed, jnp.exp(scores - newmax[..., None]), 0.0)
            factor = jnp.exp(running - newmax)
            row_total = row_total * factor + jnp.sum(exps, axis=-1)
            row_accum = row_accum * factor[..., None] + jnp.einsum(
                "kgqt,tkd->kgqd",
                exps.astype(jnp.bfloat16),
                value_block,
                preferred_element_type=jnp.float32,
            )
            return (newmax, row_total, row_accum)

        def scan_step(current, block_item):
            key_block, value_block, first_key = block_item
            updated = attend_block(current, key_block, value_block, first_key)
            return (updated, None)

        initial = (
            jnp.full((kv_local, groups, block_rows), NEG, jnp.float32),
            jnp.zeros((kv_local, groups, block_rows), jnp.float32),
            jnp.zeros((kv_local, groups, block_rows, head_size), jnp.float32),
        )
        final_state, unused = lax.scan(scan_step, initial, (key_blocks, value_blocks, firsts))
        running, row_total, row_accum = final_state
        attn_exact = row_accum / row_total[..., None]
        log_total = running + jnp.log(row_total)
        attn_local = attn_exact.transpose(2, 0, 1, 3).reshape(block_rows, -1).astype(jnp.bfloat16)
        middle = residual_in + part_sum([(attn_local, wo_use, False)])
        normed_two = (rms_scale(middle) * ffn_gain).astype(jnp.bfloat16)
        normed_two_all = rows_of((normed_two,))[0]
        gate_proj = dot_plain(normed_two_all, wg_use)
        up_proj = dot_plain(normed_two_all, wu_use)
        hidden = (jax.nn.silu(gate_proj) * up_proj).astype(jnp.bfloat16)
        out_list.append((middle + part_sum([(hidden, wd_use, False)])).astype(jnp.bfloat16))
        grad_down = dot_outer(hidden, cot_all)
        grad_hidden = dot_back(cot_all, wd_use)
        sigmoid_gate = jax.nn.sigmoid(gate_proj)
        grad_gate = (
            grad_hidden * up_proj * sigmoid_gate * (1.0 + gate_proj * (1.0 - sigmoid_gate))
        ).astype(jnp.bfloat16)
        grad_upper = (grad_hidden * gate_proj * sigmoid_gate).astype(jnp.bfloat16)
        grad_gate_w = dot_outer(normed_two_all, grad_gate)
        grad_up_w = dot_outer(normed_two_all, grad_upper)
        grad_normed_two = part_sum([(grad_gate, wg_use, True), (grad_upper, wu_use, True)])
        grad_mid_part, ffn_gain_part = norm_back(middle, ffn_gain, grad_normed_two)
        grad_middle = grad_block + grad_mid_part
        grad_attn_low = grad_middle.astype(jnp.bfloat16)
        grad_mid_all = rows_of((grad_attn_low,))[0]
        grad_output_w = dot_outer(attn_local, grad_mid_all)
        grad_attn = (
            dot_back(grad_mid_all, wo_use)
            .astype(jnp.bfloat16)
            .reshape(block_rows, kv_local, groups, head_size)
        )
        row_delta = jnp.einsum("qkgd,kgqd->kgq", grad_attn.astype(jnp.float32), attn_exact)

        def back_block(grad_query, key_block, value_block, first_key):
            scores, allowed = block_scores(
                query_here, key_block, row_pos, row_begin, first_key, starts, score_scale
            )
            probabilities = jnp.where(allowed, jnp.exp(scores - log_total[..., None]), 0.0)
            grad_value = jnp.einsum(
                "kgqt,qkgd->tkd",
                probabilities.astype(jnp.bfloat16),
                grad_attn,
                preferred_element_type=jnp.float32,
            )
            grad_probs = jnp.einsum(
                "qkgd,tkd->kgqt", grad_attn, value_block, preferred_element_type=jnp.float32
            )
            grad_scores = (probabilities * (grad_probs - row_delta[..., None])).astype(jnp.bfloat16)
            grad_query = (
                grad_query
                + jnp.einsum(
                    "kgqt,tkd->qkgd", grad_scores, key_block, preferred_element_type=jnp.float32
                )
                * score_scale
            )
            grad_key = (
                jnp.einsum(
                    "kgqt,qkgd->tkd", grad_scores, query_here, preferred_element_type=jnp.float32
                )
                * score_scale
            )
            return (grad_query, (grad_key, grad_value))

        def back_step(grad_query, block_item):
            key_block, value_block, first_key = block_item
            stepped = back_block(grad_query, key_block, value_block, first_key)
            return stepped

        grad_query, key_value_grads = lax.scan(
            back_step,
            jnp.zeros((block_rows, kv_local, groups, head_size), jnp.float32),
            (key_blocks, value_blocks, firsts),
        )
        key_mine, value_mine = (
            lax.psum_scatter(
                key_value_grads[0].reshape(total_rows, -1).astype(jnp.bfloat16),
                "seq",
                scatter_dimension=0,
                tiled=True,
            ).astype(jnp.float32),
            lax.psum_scatter(
                key_value_grads[1].reshape(total_rows, -1).astype(jnp.bfloat16),
                "seq",
                scatter_dimension=0,
                tiled=True,
            ).astype(jnp.float32),
        )
        grad_query_rot = rotate(
            grad_query.reshape(block_rows, -1, head_size), cos_table, -sin_table
        )
        grad_key_rot = rotate(key_mine.reshape(block_rows, -1, head_size), cos_table, -sin_table)
        grad_query_raw, query_gain_part = norm_back(query_raw, query_gain, grad_query_rot)
        grad_key_raw, key_gain_part = norm_back(key_raw, key_gain, grad_key_rot)
        query_low = grad_query_raw.reshape(block_rows, -1).astype(jnp.bfloat16)
        key_low = grad_key_raw.reshape(block_rows, -1).astype(jnp.bfloat16)
        value_low = value_mine.astype(jnp.bfloat16)
        grad_query_w = dot_outer(normed_all, query_low)
        grad_key_w = dot_outer(normed_all, key_low)
        grad_value_w = dot_outer(normed_all, value_low)
        grad_normed = part_sum(
            [(query_low, wq_use, True), (key_low, wk_use, True), (value_low, wv_use, True)]
        )
        grad_in_part, attn_gain_part = norm_back(residual_in, attn_gain, grad_normed)
        input_grads.append(grad_middle + grad_in_part)
        gain_totals = (
            gain_totals[0] + jnp.sum(attn_gain_part, axis=0),
            gain_totals[1] + jnp.sum(query_gain_part, axis=(0, 1)),
            gain_totals[2] + jnp.sum(key_gain_part, axis=(0, 1)),
            gain_totals[3] + jnp.sum(ffn_gain_part, axis=0),
        )
        batch_terms = (
            grad_query_w,
            grad_key_w,
            grad_value_w,
            grad_output_w,
            grad_gate_w,
            grad_up_w,
            grad_down,
        )
        if local_sums is None:
            local_sums = batch_terms
        else:
            local_sums = tuple(
                (old_part + new_part for old_part, new_part in zip(local_sums, batch_terms))
            )
    back_cols = (
        lax.all_to_all(
            local_sums[0].astype(jnp.bfloat16), "heads", split_axis=0, concat_axis=1, tiled=True
        ).astype(jnp.float32),
        lax.all_to_all(
            local_sums[1].astype(jnp.bfloat16), "heads", split_axis=0, concat_axis=1, tiled=True
        ).astype(jnp.float32),
        lax.all_to_all(
            local_sums[2].astype(jnp.bfloat16), "heads", split_axis=0, concat_axis=1, tiled=True
        ).astype(jnp.float32),
        lax.all_to_all(
            local_sums[4].astype(jnp.bfloat16), "heads", split_axis=0, concat_axis=1, tiled=True
        ).astype(jnp.float32),
        lax.all_to_all(
            local_sums[5].astype(jnp.bfloat16), "heads", split_axis=0, concat_axis=1, tiled=True
        ).astype(jnp.float32),
    )
    shard_sums = (
        lax.psum_scatter(
            back_cols[0].astype(jnp.bfloat16), "seq", scatter_dimension=0, tiled=True
        ).astype(jnp.float32),
        lax.psum_scatter(
            back_cols[1].astype(jnp.bfloat16), "seq", scatter_dimension=0, tiled=True
        ).astype(jnp.float32),
        lax.psum_scatter(
            back_cols[2].astype(jnp.bfloat16), "seq", scatter_dimension=0, tiled=True
        ).astype(jnp.float32),
        lax.psum_scatter(
            local_sums[3].astype(jnp.bfloat16), "seq", scatter_dimension=0, tiled=True
        ).astype(jnp.float32),
        lax.psum_scatter(
            back_cols[3].astype(jnp.bfloat16), "seq", scatter_dimension=0, tiled=True
        ).astype(jnp.float32),
        lax.psum_scatter(
            back_cols[4].astype(jnp.bfloat16), "seq", scatter_dimension=0, tiled=True
        ).astype(jnp.float32),
        lax.psum_scatter(
            local_sums[6].astype(jnp.bfloat16), "seq", scatter_dimension=0, tiled=True
        ).astype(jnp.float32),
    )
    gains = lax.psum(
        (gain_totals[0], gain_totals[1], gain_totals[2], gain_totals[3]), ("heads", "seq")
    )
    block_out = jnp.stack(out_list)[:, None]
    grad_inputs = jnp.stack(input_grads)[:, None]
    return (
        block_out,
        grad_inputs,
        gains[0],
        shard_sums[0],
        shard_sums[1],
        shard_sums[2],
        shard_sums[3],
        gains[1],
        gains[2],
        gains[3],
        shard_sums[4],
        shard_sums[5],
        shard_sums[6],
    )


def solution(mesh):
    return jax.shard_map(
        per_device,
        mesh=mesh,
        in_specs=(
            P(None, "seq", "heads", None),
            P(None, "seq", "heads", None),
            P(),
            P(("heads", "seq"), None),
            P(("heads", "seq"), None),
            P(("heads", "seq"), None),
            P(("heads", "seq"), None),
            P(),
            P(),
            P(),
            P(("heads", "seq"), None),
            P(("heads", "seq"), None),
            P(("heads", "seq"), None),
            P(),
        ),
        out_specs=(
            P(None, "seq", "heads", None),
            P(None, "seq", "heads", None),
            P(),
            P(("heads", "seq"), None),
            P(("heads", "seq"), None),
            P(("heads", "seq"), None),
            P(("heads", "seq"), None),
            P(),
            P(),
            P(),
            P(("heads", "seq"), None),
            P(("heads", "seq"), None),
            P(("heads", "seq"), None),
        ),
        check_vma=False,
    )
```

profile of v0, /device:TPU:0, one launch (start us, length us, event | category | flops | bytes accessed | tf_op | source)
XLA Modules:
  0.0 1626.0 jit_solution(2472400485115393135)
XLA Ops:
  7.2 24.9 %all_gather.65 = bf16[512,512]{1,0:T(8,128)(2,1)S(1)} all-gather(bf16[32,512]{1,0:T(8,128)(2,1)} %param.26), channel_id=1, replica_groups=mesh['heads'=2,'seq'=16] {'seq'}, dimensions={0}, use_global_device_ids=true | all-gather | bytes 557056 | tf_op jit(solution)/shard_map/all_gather | solution.py:153
  38.6 12.6 all_gather.64
  51.3 8.4 all_gather.75
  63.2 18.9 %all_gather.68 = bf16[512,512]{1,0:T(8,128)(2,1)S(1)} all-gather(bf16[32,512]{1,0:T(8,128)(2,1)S(1)} %copy-done.108), channel_id=1, replica_groups=mesh['heads'=2,'seq'=16] {'seq'}, dimensions={0}, use_global_device_ids=true | all-gather | bytes 557056 | tf_op jit(solution)/shard_map/all_gather | solution.py:154
  82.4 11.2 all_to_all.215
  106.0 12.0 all-to-all-done.1
  126.9 35.7 %all-gather.28.cloned.1.call-done = bf16[4096,256]{1,0:T(8,128)(2,1)} async-done(((bf16[256,256]{1,0:T(8,128)(2,1)}), bf16[4096,256]{1,0:T(8,128)(2,1)}) %all-gather.28.cloned.1.call-update) | async-done | bytes 2097168 | tf_op jit(solution)/shard_map/all_gather | solution.py:185
  162.6 7.1 reshape.530
  169.7 7.0 copy.265
  176.7 98.2 %while.60 = (s32[]{:T(128)}, f32[4,2,256]{2,1,0:T(2,128)S(1)}, f32[4,2,256]{2,1,0:T(2,128)S(1)}, f32[4,2,256,64]{2,3,1,0:T(8,128)S(1)}, s32[8]{0:T(128)}, /*inde...) while((s32[]{:T(128)}, f32[4,2,256]{2,1,0:T(2,128)S(1)}, ...), condition=%wide.region_8.9_spmd.clone, body=%wide.region_4.8_spmd.clone.sunk | while | flops 282868480 | bytes 31864020 | solution.py:219
  279.7 7.1 reshape.531
  286.8 7.0 copy.272
  297.0 94.3 %while.61 = (s32[]{:T(128)}, f32[4,2,256]{2,1,0:T(2,128)S(1)}, f32[4,2,256]{2,1,0:T(2,128)S(1)}, f32[4,2,256,64]{2,3,1,0:T(8,128)S(1)}, s32[8]{0:T(128)}, /*inde...) while((s32[]{:T(128)}, f32[4,2,256]{2,1,0:T(2,128)S(1)}, ...), condition=%wide.region_20.21_spmd.clone, body=%wide.region_16.20_spmd.clone.sunk | while | flops 282868480 | bytes 31864020 | solution.py:219
  393.5 6.7 copy.266
  400.2 6.0 all-to-all-start.3
  406.2 6.7 copy.268
  412.9 53.9 %all-to-all-done.3 = bf16[512,2,2304]{0,2,1:T(8,128)(2,1)} async-done(((bf16[512,2,2304]{0,2,1:T(8,128)(2,1)}), bf16[512,2,2304]{0,2,1:T(8,128)(2,1)}, u32[]{:S(2)}, u32[]{:S(2)}) %all-to-all-start.3) | async-done | bytes 4718624 | tf_op jit(solution)/shard_map/all_to_all | solution.py:164
  466.8 5.9 all-to-all-start.4
  472.8 58.8 %all-gather.2 = bf16[1,1,256,1024]{3,2,1,0:T(8,128)(2,1)} all-gather(bf16[1,1,128,1024]{3,2,1,0:T(8,128)(2,1)S(1)} %get-tuple-element.1068), channel_id=4, replica_groups=mesh['heads'=2,'seq'=16] {'heads'}, dimensions={2}, use_global_device_ids=true | all-gather | bytes 786432 | tf_op jit(solution)/shard_map/all_gather | solution.py:89
  531.7 8.0 all-gather.3
  542.2 7.0 all_gather.71
  549.3 7.1 all_gather.78
  556.4 6.8 copy.267
  563.2 6.8 copy.269
  569.9 5.3 fusion.189
  583.7 7.0 multiply_convert_fusion.2
  600.2 7.0 multiply_convert_fusion
  616.6 4.9 convolution_convert_fusion
  622.8 9.5 reduce-scatter.36.cloned.1.call-done
  634.3 15.2 reduce-scatter.26.cloned.1.call-done
  651.9 8.9 all_gather.80
  666.0 108.1 %while.62 = (s32[]{:T(128)}, f32[256,4,2,64]{0,3,2,1:T(8,128)}, bf16[8,512,4,64]{1,3,2,0:T(8,128)(2,1)}, bf16[8,512,4,64]{1,3,2,0:T(8,128)(2,1)}, bf16[8,512,4,6...) while((s32[]{:T(128)}, f32[256,4,2,64]{0,3,2,1:T(8,128)}, ...), condition=%wide.region_28.29_spmd.clone, body=%wide.region_26.28_spmd.clone.sunk | while | flops 684593920 | bytes 56862064 | solution.py:288
  774.1 8.4 all_gather.82
  792.9 96.0 %while.63 = (s32[]{:T(128)}, f32[256,4,2,64]{0,3,2,1:T(8,128)S(1)}, bf16[8,512,4,64]{1,3,2,0:T(8,128)(2,1)}, bf16[8,512,4,64]{1,3,2,0:T(8,128)(2,1)}, bf16[8,512...) while((s32[]{:T(128)}, f32[256,4,2,64]{0,3,2,1:T(8,128)S(1)}, ...), condition=%wide.region_39.40_spmd.clone, body=%wide.region_37.39_spmd.clone.sunk | while | flops 684593920 | bytes 56792336 | solution.py:288
  914.6 9.6 all-to-all-done.5
  927.8 27.8 %reduce-scatter.38.cloned.1.call-done = bf16[256,256]{0,1:T(8,128)(2,1)} async-done(((bf16[4096,256]{0,1:T(8,128)(2,1)}), bf16[256,256]{0,1:T(8,128)(2,1)}) %reduce-scatter.38.cloned.1.call-update) | async-done | bytes 131088 | tf_op jit(solution)/shard_map/reduce_scatter | solution.py:294
  963.2 57.1 %reduce-scatter.32.cloned.1.call-done = bf16[256,256]{0,1:T(8,128)(2,1)} async-done(((bf16[4096,256]{0,1:T(8,128)(2,1)}), bf16[256,256]{0,1:T(8,128)(2,1)}) %reduce-scatter.32.cloned.1.call-update) | async-done | bytes 131088 | tf_op jit(solution)/shard_map/reduce_scatter | solution.py:300
  1023.7 60.8 %reduce-scatter.40.cloned.1.call-done = bf16[256,256]{0,1:T(8,128)(2,1)} async-done(((bf16[4096,256]{0,1:T(8,128)(2,1)}), bf16[256,256]{0,1:T(8,128)(2,1)}) %reduce-scatter.40.cloned.1.call-update) | async-done | bytes 131088 | tf_op jit(solution)/shard_map/reduce_scatter | solution.py:300
  1087.4 9.3 all_to_all.216
  1098.3 9.0 all_to_all.217
  1122.6 52.2 %all_to_all.218 = bf16[2,512,2304]{2,1,0:T(8,128)(2,1)S(1)} all-to-all(bf16[2,512,2304]{2,1,0:T(8,128)(2,1)S(1)} %bitcast.610), channel_id=1, replica_groups=mesh['heads'=2,'seq'=16] {'heads'}, dimensions={0} | all-to-all | bytes 9437184 | tf_op jit(solution)/shard_map/all_to_all | solution.py:355
  1181.5 57.5 %all_to_all.219 = bf16[2,512,2304]{2,1,0:T(8,128)(2,1)S(1)} all-to-all(bf16[2,512,2304]{2,1,0:T(8,128)(2,1)S(1)} %bitcast.609), channel_id=1, replica_groups=mesh['heads'=2,'seq'=16] {'heads'}, dimensions={0} | all-to-all | bytes 9437184 | tf_op jit(solution)/shard_map/all_to_all | solution.py:358
  1246.9 58.0 %reduce-scatter.46.cloned.1.call-done = bf16[32,512]{1,0:T(8,128)(2,1)} async-done(((bf16[512,512]{1,0:T(8,128)(2,1)}), bf16[32,512]{1,0:T(8,128)(2,1)}) %reduce-scatter.46.cloned.1.call-update) | async-done | bytes 32784 | tf_op jit(solution)/shard_map/reduce_scatter | solution.py:366
  1306.3 57.5 %reduce-scatter.48.cloned.1.call-done = bf16[32,512]{1,0:T(8,128)(2,1)} async-done(((bf16[512,512]{1,0:T(8,128)(2,1)}), bf16[32,512]{1,0:T(8,128)(2,1)}) %reduce-scatter.48.cloned.1.call-update) | async-done | bytes 32784 | tf_op jit(solution)/shard_map/reduce_scatter | solution.py:369
  1365.2 40.2 %all-reduce = (f32[1024]{0:T(1024)}, f32[64]{0:T(128)}, f32[64]{0:T(128)}, f32[1024]{0:T(1024)}) all-reduce(f32[1024]{0:T(1024)S(1)} %add.380, f32[64]{0:T(128)S(1)} %add.385, f32[64]{0:T(128)S(1)} %add.386, f32[1024]{0:T(1024)S(1)} %add.387), channel_id=1, replica_groups=mesh['heads'=2,'seq'=16] {'heads','seq'}, use_global_device_ids=true, to_apply=%region_48.49 | all-reduce | flops 2176 | bytes 17408 | tf_op jit(solution)/shard_map/psum | solution.py:385
  1409.4 50.4 %reduce-scatter.56.cloned.1.call-done = bf16[144,1024]{1,0:T(8,128)(2,1)} async-done(((bf16[2304,1024]{1,0:T(8,128)(2,1)}), bf16[144,1024]{1,0:T(8,128)(2,1)}) %reduce-scatter.56.cloned.1.call-update) | async-done | bytes 294928 | tf_op jit(solution)/shard_map/reduce_scatter | solution.py:381
  1461.7 77.0 %reduce-scatter.52.cloned.1.call-done = bf16[32,4608]{1,0:T(8,128)(2,1)} async-done(((bf16[512,4608]{1,0:T(8,128)(2,1)}), bf16[32,4608]{1,0:T(8,128)(2,1)}) %reduce-scatter.52.cloned.1.call-update) | async-done | bytes 294928 | tf_op jit(solution)/shard_map/reduce_scatter | solution.py:375
  1540.5 76.7 %reduce-scatter.54.cloned.1.call-done = bf16[32,4608]{1,0:T(8,128)(2,1)} async-done(((bf16[512,4608]{1,0:T(8,128)(2,1)}), bf16[32,4608]{1,0:T(8,128)(2,1)}) %reduce-scatter.54.cloned.1.call-update) | async-done | bytes 294928 | tf_op jit(solution)/shard_map/reduce_scatter | solution.py:378
  (964 shorter events, 572.4 us)
Async XLA Ops:
  33.4 27.4 %all-to-all-start = ((bf16[512,2,256]{2,0,1:T(8,128)(2,1)}), bf16[512,2,256]{2,0,1:T(8,128)(2,1)S(1)}, u32[]{:S(2)}, u32[]{:S(2)}) async-start(bf16[512,2,256]{2,0,1:T(8,128)(2,1)} %copy.256), calls=%async_computation | async-start | bytes 1048576 | tf_op jit(solution)/shard_map/all_to_all | solution.py:162
  36.9 61.1 %all-gather.16.cloned.1.call-start = ((), (), s32[]{:S(2)}) async-start(), calls=%async_computation.30 | async-start | bytes 1114112 | tf_op jit(solution)/shard_map/all_gather | solution.py:152
  37.6 84.8 %all-gather.14.cloned.1.call-start = ((), (), s32[]{:S(2)}) async-start(), calls=%async_computation.29 | async-start | bytes 2228224 | tf_op jit(solution)/shard_map/all_gather | solution.py:184
  63.1 99.5 %all-gather.28.cloned.1.call-start = ((), (), s32[]{:S(2)}) async-start(), calls=%async_computation.55 | async-start | bytes 2228224 | tf_op jit(solution)/shard_map/all_gather | solution.py:185
  94.8 180.2 %all-gather.26.cloned.1.call-start = ((), (), s32[]{:S(2)}) async-start(), calls=%async_computation.37 | async-start | bytes 2228224 | tf_op jit(solution)/shard_map/all_gather | solution.py:184
  95.6 184.1 %all-gather.30.cloned.1.call-start = ((), (), s32[]{:S(2)}) async-start(), calls=%async_computation.56 | async-start | bytes 2228224 | tf_op jit(solution)/shard_map/all_gather | solution.py:185
  96.6 197.2 %all-gather.18.cloned.1.call-start = ((), (), s32[]{:S(2)}) async-start(), calls=%async_computation.31 | async-start | bytes 1114112 | tf_op jit(solution)/shard_map/all_gather | solution.py:155
  97.2 296.3 %all-gather.20.cloned.1.call-start = ((), (), s32[]{:S(2)}) async-start(), calls=%async_computation.33 | async-start | bytes 5013504 | tf_op jit(solution)/shard_map/all_gather | solution.py:156
  100.8 17.2 %all-to-all-start.1 = ((bf16[512,2,512]{2,0,1:T(8,128)(2,1)}), bf16[512,2,512]{2,0,1:T(8,128)(2,1)S(1)}, u32[]{:S(2)}, u32[]{:S(2)}) async-start(bf16[512,2,512]{2,0,1:T(8,128)(2,1)} %copy.259), calls=%async_computation.1 | async-start | bytes 2097152 | tf_op jit(solution)/shard_map/all_to_all | solution.py:161
  104.4 301.8 %all-gather.22.cloned.1.call-start = ((), (), s32[]{:S(2)}) async-start(), calls=%async_computation.34 | async-start | bytes 5013504 | tf_op jit(solution)/shard_map/all_gather | solution.py:157
  105.1 434.5 %reduce-scatter.20.cloned.1.call-start = ((), (), s32[]{:S(2)}) async-start(), calls=%async_computation.32 | async-start | bytes 786432 | tf_op jit(solution)/shard_map/reduce_scatter | solution.py:101
  296.4 243.2 %reduce-scatter.24.cloned.1.call-start = ((), (), s32[]{:S(2)}) async-start(), calls=%async_computation.38 | async-start | bytes 786432 | tf_op jit(solution)/shard_map/reduce_scatter | solution.py:101
  296.9 94.5 %copy-start.13 = (bf16[512,1024]{1,0:T(8,128)(2,1)S(1)}, bf16[512,1024]{1,0:T(8,128)(2,1)}, u32[]{:S(2)}) copy-start(bf16[512,1024]{1,0:T(8,128)(2,1)} %all-gather.18.cloned.1.call-done) | copy-start | bytes 3145732
  392.7 191.0 %all-gather.24.cloned.1.call-start = ((), (), s32[]{:S(2)}) async-start(), calls=%async_computation.35 | async-start | bytes 5013504 | tf_op jit(solution)/shard_map/all_gather | solution.py:158
  400.2 66.6 %all-to-all-start.3 = ((bf16[512,2,2304]{0,2,1:T(8,128)(2,1)}), bf16[512,2,2304]{0,2,1:T(8,128)(2,1)}, u32[]{:S(2)}, u32[]{:S(2)}) async-start(bf16[512,2,2304]{0,2,1:T(8,128)(2,1)} %bitcast.606), calls=%async_computation.4 | async-start | bytes 9437184 | tf_op jit(solution)/shard_map/all_to_all | solution.py:164
  466.8 96.3 %all-to-all-start.4 = ((bf16[512,2,2304]{0,2,1:T(8,128)(2,1)}), bf16[512,2,2304]{0,2,1:T(8,128)(2,1)}, u32[]{:S(2)}, u32[]{:S(2)}) async-start(bf16[512,2,2304]{0,2,1:T(8,128)(2,1)} %bitcast.605), calls=%async_computation.5 | async-start | bytes 9437184 | tf_op jit(solution)/shard_map/all_to_all | solution.py:165
  472.7 150.0 %reduce-scatter.28.cloned.1.call-start = ((), (), s32[]{:S(2)}) async-start(), calls=%async_computation.40 | async-start | bytes 786432 | tf_op jit(solution)/shard_map/reduce_scatter | solution.py:101
  540.9 108.6 %copy-start.117 = (f32[128]{0:T(128)}, f32[128]{0:T(128)S(1)}, u32[]{:S(2)}) copy-start(f32[128]{0:T(128)S(1)} %add_rsqrt_fusion.6) | copy-start | bytes 1540
  541.0 108.5 %copy-start.115 = (f32[128]{0:T(128)}, f32[128]{0:T(128)S(1)}, u32[]{:S(2)}) copy-start(f32[128]{0:T(128)S(1)} %add_rsqrt_fusion.4) | copy-start | bytes 1540
  600.0 32.3 %reduce-scatter.36.cloned.1.call-start = ((), (), s32[]{:S(2)}) async-start(), calls=%async_computation.44 | async-start | bytes 786432 | tf_op jit(solution)/shard_map/reduce_scatter | solution.py:101
  616.5 33.0 %reduce-scatter.26.cloned.1.call-start = ((), (), s32[]{:S(2)}) async-start(), calls=%async_computation.39 | async-start | bytes 786432 | tf_op jit(solution)/shard_map/reduce_scatter | solution.py:101
  621.5 303.9 %reduce-scatter.30.cloned.1.call-start = ((), (), s32[]{:S(2)}) async-start(), calls=%async_computation.41 | async-start | bytes 2228224 | tf_op jit(solution)/shard_map/reduce_scatter | solution.py:294
  789.8 165.8 %reduce-scatter.38.cloned.1.call-start = ((), (), s32[]{:S(2)}) async-start(), calls=%async_computation.45 | async-start | bytes 2228224 | tf_op jit(solution)/shard_map/reduce_scatter | solution.py:294
  894.0 126.3 %reduce-scatter.32.cloned.1.call-start = ((), (), s32[]{:S(2)}) async-start(), calls=%async_computation.42 | async-start | bytes 2228224 | tf_op jit(solution)/shard_map/reduce_scatter | solution.py:300
  897.5 187.0 %reduce-scatter.40.cloned.1.call-start = ((), (), s32[]{:S(2)}) async-start(), calls=%async_computation.46 | async-start | bytes 2228224 | tf_op jit(solution)/shard_map/reduce_scatter | solution.py:300
  901.5 340.8 %reduce-scatter.50.cloned.1.call-start = ((), (), s32[]{:S(2)}) async-start(), calls=%async_computation.51 | async-start | bytes 1114112 | tf_op jit(solution)/shard_map/reduce_scatter | solution.py:372
  908.5 15.6 all-to-all-start.5
  912.1 331.7 %reduce-scatter.44.cloned.1.call-start = ((), (), s32[]{:S(2)}) async-start(), calls=%async_computation.48 | async-start | bytes 1114112 | tf_op jit(solution)/shard_map/reduce_scatter | solution.py:363
  925.3 320.1 %reduce-scatter.34.cloned.1.call-start = ((), (), s32[]{:S(2)}) async-start(), calls=%async_computation.43 | async-start | bytes 786432 | tf_op jit(solution)/shard_map/reduce_scatter | solution.py:101
  1022.8 222.6 %reduce-scatter.42.cloned.1.call-start = ((), (), s32[]{:S(2)}) async-start(), calls=%async_computation.47 | async-start | bytes 786432 | tf_op jit(solution)/shard_map/reduce_scatter | solution.py:101
  1086.6 218.3 %reduce-scatter.46.cloned.1.call-start = ((), (), s32[]{:S(2)}) async-start(), calls=%async_computation.49 | async-start | bytes 557056 | tf_op jit(solution)/shard_map/reduce_scatter | solution.py:366
  1097.5 266.3 %reduce-scatter.48.cloned.1.call-start = ((), (), s32[]{:S(2)}) async-start(), calls=%async_computation.50 | async-start | bytes 557056 | tf_op jit(solution)/shard_map/reduce_scatter | solution.py:369
  1108.2 297.3 %reduce-scatter.22.cloned.1.call-start = ((), (), s32[]{:S(2)}) async-start(), calls=%async_computation.36 | async-start | bytes 786432 | tf_op jit(solution)/shard_map/reduce_scatter | solution.py:101
  1112.9 347.0 %reduce-scatter.56.cloned.1.call-start = ((), (), s32[]{:S(2)}) async-start(), calls=%async_computation.54 | async-start | bytes 5013504 | tf_op jit(solution)/shard_map/reduce_scatter | solution.py:381
  1118.2 420.4 %reduce-scatter.52.cloned.1.call-start = ((), (), s32[]{:S(2)}) async-start(), calls=%async_computation.52 | async-start | bytes 5013504 | tf_op jit(solution)/shard_map/reduce_scatter | solution.py:375
  1177.4 439.8 %reduce-scatter.54.cloned.1.call-start = ((), (), s32[]{:S(2)}) async-start(), calls=%async_computation.53 | async-start | bytes 5013504 | tf_op jit(solution)/shard_map/reduce_scatter | solution.py:378
  1241.7 163.8 %copy-start.26 = (bf16[128,1024]{1,0:T(8,128)(2,1)S(1)}, bf16[128,1024]{1,0:T(8,128)(2,1)}, u32[]{:S(2)}) copy-start(bf16[128,1024]{1,0:T(8,128)(2,1)} %reduce-scatter.20.cloned.1.call-done) | copy-start | bytes 786436
  1241.7 163.8 %copy-start.41 = (bf16[2,1,128,1024]{3,2,1,0:T(8,128)(2,1)S(1)}, bf16[2,1,128,1024]{3,2,1,0:T(8,128)(2,1)}, u32[]{:S(2)}) copy-start(bf16[2,1,128,1024]{3,2,1,0:T(8,128)(2,1)} %param.23) | copy-start | bytes 1572868
  1241.7 163.8 %copy-start.52 = (bf16[128,1024]{1,0:T(8,128)(2,1)S(1)}, bf16[128,1024]{1,0:T(8,128)(2,1)}, u32[]{:S(2)}) copy-start(bf16[128,1024]{1,0:T(8,128)(2,1)} %reduce-scatter.28.cloned.1.call-done) | copy-start | bytes 786436
  1241.7 163.8 %copy-start.99 = (f32[1024]{0:T(1024)S(1)}, f32[1024]{0:T(1024)}, u32[]{:S(2)}) copy-start(f32[1024]{0:T(1024)} %param.31) | copy-start | bytes 12292
  1241.7 163.8 %copy-start.118 = (f32[128]{0:T(128)S(1)}, f32[128]{0:T(128)}, u32[]{:S(2)}) copy-start(f32[128]{0:T(128)} %copy-done.117) | copy-start | bytes 1540
  1241.7 163.8 %copy-start.130 = (f32[128]{0:T(128)S(1)}, f32[128]{0:T(128)}, u32[]{:S(2)}) copy-start(f32[128]{0:T(128)} %copy-done.129) | copy-start | bytes 1540
  1241.8 165.3 %copy-start.80 = (bf16[1,128,1024]{2,1,0:T(8,128)(2,1)S(1)}, bf16[1,128,1024]{2,1,0:T(8,128)(2,1)}, u32[]{:S(2)}) copy-start(bf16[1,128,1024]{2,1,0:T(8,128)(2,1)} %get-tuple-element.1052) | copy-start | bytes 786436
  1245.3 162.5 %copy-start.24 = (bf16[128,1024]{1,0:T(8,128)(2,1)S(1)}, bf16[128,1024]{1,0:T(8,128)(2,1)}, u32[]{:S(2)}) copy-start(bf16[128,1024]{1,0:T(8,128)(2,1)} %reduce-scatter.24.cloned.1.call-done) | copy-start | bytes 786436
  1245.3 162.5 %copy-start.51 = (bf16[128,1024]{1,0:T(8,128)(2,1)S(1)}, bf16[128,1024]{1,0:T(8,128)(2,1)}, u32[]{:S(2)}) copy-start(bf16[128,1024]{1,0:T(8,128)(2,1)} %reduce-scatter.36.cloned.1.call-done) | copy-start | bytes 786436
  1245.3 162.5 %copy-start.116 = (f32[128]{0:T(128)S(1)}, f32[128]{0:T(128)}, u32[]{:S(2)}) copy-start(f32[128]{0:T(128)} %copy-done.115) | copy-start | bytes 1540
  1245.3 162.5 %copy-start.128 = (f32[128]{0:T(128)S(1)}, f32[128]{0:T(128)}, u32[]{:S(2)}) copy-start(f32[128]{0:T(128)} %copy-done.127) | copy-start | bytes 1540
  1245.5 162.4 %copy-start.79 = (bf16[128,1024]{1,0:T(8,128)(2,1)S(1)}, bf16[128,1024]{1,0:T(8,128)(2,1)}, u32[]{:S(2)}) copy-start(bf16[128,1024]{1,0:T(8,128)(2,1)} %reduce-scatter.42.cloned.1.call-done) | copy-start | bytes 786436
  (185 other events, 1624.8 us)
Sparse Core Ops, SparseCore 0:
  39.9 36.9 all-gather.15
  79.6 39.8 all-gather.13
  122.3 40.3 all-gather.27
  165.2 39.9 all-gather.25
  207.8 40.3 all-gather.29
  250.2 36.6 all-gather.17
  289.2 52.1 all-gather.19
  343.7 51.8 all-gather.21
  398.4 14.4 reduce-scatter.19
  415.6 22.4 reduce-scatter.23
  440.4 53.2 all-gather.23
  600.1 14.6 reduce-scatter.27
  617.7 14.5 reduce-scatter.35
  634.9 14.5 reduce-scatter.25
  789.9 61.5 reduce-scatter.29
  894.1 61.4 reduce-scatter.37
  959.7 60.5 reduce-scatter.31
  1023.9 60.5 reduce-scatter.39
  1088.6 56.3 reduce-scatter.49
  1148.5 56.3 reduce-scatter.43
  1207.8 19.3 reduce-scatter.33
  1230.0 14.9 reduce-scatter.41
  1249.5 55.3 reduce-scatter.45
  1308.9 54.8 reduce-scatter.47
  1366.7 13.6 reduce-scatter.21
  1384.1 75.6 reduce-scatter.55
  1464.0 74.5 reduce-scatter.51
  1542.5 74.5 reduce-scatter.53
where the time goes:
time: 1640 us; the launch traced here: 1630 us
  waiting for transfers between devices  605 us (37%)
  blocking collectives  343 us (21%)
  matrix products  343 us (21%)
  local copies, waits for them, and re-layouts  158 us (10%)
  other arithmetic  134 us (8%)
  starting transfers between devices  25.2 us (2%)
  between operations  16.5 us (1%)
    all_gather x8, blocking collectives, rows_of(): lax.all_gather(as_sent(parts), 'heads', axis=0, tiled=True)  119 us
    reduce_scatter x2, waiting for transfers between devices, per_device(): lax.psum_scatter(key_value_grads[1].reshape(total_rows, -1).astype(jnp.bf...  118 us
    dot_general x32, matrix products, block_scores(): jnp.einsum('qkgd,tkd->kgqt', query_here, key_block, preferred_element_typ...  87.5 us
    reduce_scatter x1, waiting for transfers between devices, per_device(): lax.psum_scatter(back_cols[3].astype(jnp.bfloat16), 'seq', scatter_dimens...  77 us
    reduce_scatter x1, waiting for transfers between devices, per_device(): lax.psum_scatter(back_cols[4].astype(jnp.bfloat16), 'seq', scatter_dimens...  76.7 us
    reduce_scatter x1, waiting for transfers between devices, per_device(): lax.psum_scatter(back_cols[1].astype(jnp.bfloat16), 'seq', scatter_dimens...  58 us
    all_to_all x1, blocking collectives, per_device(): lax.all_to_all(local_sums[5].astype(jnp.bfloat16), 'heads', split_axis=0,...  57.5 us
    reduce_scatter x1, waiting for transfers between devices, per_device(): lax.psum_scatter(back_cols[2].astype(jnp.bfloat16), 'seq', scatter_dimens...  57.5 us
  transfers between devices with their start and end apart: 33, of which 14 were waited for; matrix products, arithmetic and copies ran while one was open for 30% of the time, Pallas kernels for 0%

commit v1 on v0

v1 whole, which is shorter than its diff:
```python
import functools
import math

import jax
import jax.numpy as jnp
from jax import lax
from jax.experimental import pallas as pl
from jax.experimental.pallas import tpu as pltpu
from jax.sharding import Mesh, PartitionSpec as P

EPS = 1e-05
THETA = 1000000.0
LANES = 128
LOG2E = math.log2(math.e)
GROUP = ("heads", "mid")
DATA = ("hi", "lo")
SEQ = ("hi", "mid", "lo")
ALL = ("heads",) + SEQ
BF = jnp.bfloat16
F32 = jnp.float32
VMEM_LIMIT = 48 * 1024 * 1024


def dot_plain(left_side, right_side):
    return jnp.dot(left_side, right_side, preferred_element_type=F32)


def dot_back(left_side, right_side):
    return lax.dot_general(
        left_side, right_side, (((1,), (1,)), ((), ())), preferred_element_type=F32
    )


def dot_outer(left_side, right_side):
    return lax.dot_general(
        left_side, right_side, (((0,), (0,)), ((), ())), preferred_element_type=F32
    )


def rms_inverse(values):
    return lax.rsqrt(jnp.mean(values * values, axis=-1, keepdims=True) + EPS)


def norm_back(values, gain_vec, upstream):
    inverse = rms_inverse(values)
    scaled = upstream * gain_vec
    inner_mean = jnp.mean(scaled * values, axis=-1, keepdims=True)
    grad_values = inverse * scaled - values * inverse * inverse * inverse * inner_mean
    return (grad_values, upstream * values * inverse)


def is_quad():
    return lax.axis_size("heads") == 2 and lax.axis_size("mid") == 2


def swap(part, axis):
    return lax.ppermute(part, axis, [(0, 1), (1, 0)])


def group_gather(part):
    if not is_quad():
        return lax.all_gather(part, GROUP, axis=0, tiled=False)
    half = part.shape[0] // 2
    by_mid = swap(part, "mid")
    by_heads = swap(part, "heads")
    far_low = swap(by_mid[:half], "heads")
    far_high = swap(by_heads[half:], "mid")
    return jnp.stack([part, by_mid, by_heads, jnp.concatenate([far_low, far_high], axis=0)])


def group_sum(parts):
    if not is_quad():
        return lax.psum_scatter(parts, GROUP, scatter_dimension=0, tiled=False).astype(F32)
    half = parts.shape[1] // 2
    far_low = swap(parts[3, :half], "mid")
    far_high = swap(parts[3, half:], "heads")
    for_mid = jnp.concatenate(
        [parts[1, :half], (parts[1, half:].astype(F32) + far_high.astype(F32)).astype(BF)], axis=0
    )
    for_heads = jnp.concatenate(
        [(parts[2, :half].astype(F32) + far_low.astype(F32)).astype(BF), parts[2, half:]], axis=0
    )
    by_mid = swap(for_mid, "mid")
    by_heads = swap(for_heads, "heads")
    return parts[0].astype(F32) + by_mid.astype(F32) + by_heads.astype(F32)


def slot_places():
    head_at = lax.axis_index("heads")
    mid_at = lax.axis_index("mid")
    if is_quad():
        return (
            jnp.stack([head_at, head_at, 1 - head_at, 1 - head_at]),
            jnp.stack([mid_at, 1 - mid_at, mid_at, 1 - mid_at]),
        )
    mids = lax.axis_size("mid")
    slots = jnp.arange(lax.axis_size("heads") * mids, dtype=jnp.int32)
    return (slots // mids, slots % mids)


def all_sum(vector):
    for axis in ("lo", "mid", "heads", "hi"):
        size = lax.axis_size(axis)
        if size & (size - 1):
            vector = lax.psum(vector, axis)
            continue
        step = 1
        while step < size:
            vector = vector + lax.ppermute(vector, axis, [(i, i ^ step) for i in range(size)])
            step *= 2
    return vector


def columns_out(parts):
    return lax.all_to_all(
        parts.transpose(1, 0, 2), GROUP, split_axis=0, concat_axis=0, tiled=True
    )


def gather_data(part):
    return lax.all_gather(part, DATA, axis=0, tiled=False)


def natural_rows(gathered):
    heads, mids = lax.axis_size("heads"), lax.axis_size("mid")
    his, los = lax.axis_size("hi"), lax.axis_size("lo")
    rows, cols = gathered.shape[2:]
    parts = gathered.reshape(his, los, heads, mids, rows, cols)
    return parts.transpose(2, 0, 3, 1, 4, 5).reshape(-1, cols)


def scatter_rows(grads):
    heads, mids = lax.axis_size("heads"), lax.axis_size("mid")
    his, los = lax.axis_size("hi"), lax.axis_size("lo")
    cols = grads.shape[1]
    parts = grads.reshape(heads, his, mids, los, -1, cols).transpose(1, 3, 0, 2, 4, 5)
    rows = parts.shape[4]
    summed = lax.psum_scatter(
        parts.reshape(his * los, heads * mids * rows, cols),
        DATA,
        scatter_dimension=0,
        tiled=False,
    )
    return summed.reshape(heads * mids, rows, cols)


def row_moves():
    mids, los = lax.axis_size("mid"), lax.axis_size("lo")
    count = lax.axis_size("hi") * mids * los
    share = count // mids
    moves = []
    for source in range(count):
        owner, rest = source // share, source % share
        moves.append((source, ((rest // los) * mids + owner) * los + rest % los))
    return moves


def rows_out(part):
    return lax.ppermute(part, SEQ, row_moves())


def rows_back(part):
    return lax.ppermute(part, SEQ, [(there, here) for here, there in row_moves()])


def lane_index(shape):
    return lax.broadcasted_iota(jnp.int32, shape, len(shape) - 1)


def half_sums(values, lane, head_size):
    first = jnp.sum(jnp.where(lane < head_size, values, 0.0), axis=-1, keepdims=True)
    second = jnp.sum(jnp.where(lane < head_size, 0.0, values), axis=-1, keepdims=True)
    return jnp.where(lane < head_size, first, second)


def partner(values, lane, head_size):
    quarter = head_size // 2
    return jnp.where(
        lane % head_size < quarter,
        pltpu.roll(values, LANES - quarter, 1),
        pltpu.roll(values, quarter, 1),
    )


def project_kernel(
    head_size, normed_ref, w_ref, cos_ref, sin_ref, qgain_ref, kgain_ref, raw_ref, q_ref, kv_ref
):
    raw = dot_plain(normed_ref[...], w_ref[...])
    raw_ref[...] = raw
    cos, sin = cos_ref[...], sin_ref[...]
    lane = lane_index(cos.shape)
    q_width = q_ref.shape[1]
    for at in range(0, raw.shape[1], LANES):
        part = raw[:, at : at + LANES]
        is_query = at < q_width
        inverse = lax.rsqrt(half_sums(part * part, lane, head_size) / head_size + EPS)
        scaled = part * inverse * (qgain_ref[...] if is_query else kgain_ref[...])
        turned = scaled * cos + partner(scaled, lane, head_size) * sin
        if is_query:
            q_ref[:, at : at + LANES] = turned.astype(BF)
        else:
            out_at = at - q_width
            kv_ref[:, out_at : out_at + LANES] = jnp.where(lane < head_size, turned, part).astype(BF)


def project(normed, w_qkv, cos, sin, query_gain, key_gain, q_width, head_size):
    rows, width = normed.shape
    cols = w_qkv.shape[1]
    tile = 256
    whole = lambda i: (0, 0)
    step = lambda i: (i, 0)
    return pl.pallas_call(
        functools.partial(project_kernel, head_size),
        grid=(rows // tile,),
        in_specs=[
            pl.BlockSpec((tile, width), step),
            pl.BlockSpec((width, cols), whole),
            pl.BlockSpec((tile, LANES), step),
            pl.BlockSpec((tile, LANES), step),
            pl.BlockSpec((1, LANES), whole),
            pl.BlockSpec((1, LANES), whole),
        ],
        out_specs=[
            pl.BlockSpec((tile, cols), step),
            pl.BlockSpec((tile, q_width), step),
            pl.BlockSpec((tile, cols - q_width), step),
        ],
        out_shape=[
            jax.ShapeDtypeStruct((rows, cols), F32),
            jax.ShapeDtypeStruct((rows, q_width), BF),
            jax.ShapeDtypeStruct((rows, cols - q_width), BF),
        ],
        compiler_params=pltpu.CompilerParams(vmem_limit_bytes=VMEM_LIMIT),
    )(normed, w_qkv, cos, sin, query_gain, key_gain)


def unproject_kernel(
    head_size, raw_ref, dq_ref, dkv_ref, cos_ref, sin_ref, qgain_ref, kgain_ref, out_ref, gain_ref
):
    cos, sin = cos_ref[...], sin_ref[...]
    lane = lane_index(cos.shape)
    q_width = dq_ref.shape[1]
    totals = [jnp.zeros((1, LANES), F32), jnp.zeros((1, LANES), F32)]
    for at in range(0, raw_ref.shape[1], LANES):
        part = raw_ref[:, at : at + LANES]
        is_query = at < q_width
        if is_query:
            upstream = dq_ref[:, at : at + LANES]
            gain = qgain_ref[...]
        else:
            upstream = dkv_ref[:, at - q_width : at - q_width + LANES].astype(F32)
            gain = kgain_ref[...]
        turned = upstream * cos - partner(upstream, lane, head_size) * sin
        inverse = lax.rsqrt(half_sums(part * part, lane, head_size) / head_size + EPS)
        scaled = turned * gain
        inner = half_sums(scaled * part, lane, head_size) / head_size
        grad = inverse * scaled - part * inverse * inverse * inverse * inner
        gain_part = jnp.sum(turned * part * inverse, axis=0, keepdims=True)
        if not is_query:
            grad = jnp.where(lane < head_size, grad, upstream)
            gain_part = jnp.where(lane[:1] < head_size, gain_part, 0.0)
        totals[0 if is_query else 1] += gain_part
        out_ref[:, at : at + LANES] = grad.astype(BF)
    gain_ref[0] = jnp.concatenate(totals, axis=0)


def unproject(raw, dq, dkv, cos, sin, query_gain, key_gain, head_size):
    rows, cols = raw.shape
    q_width = dq.shape[1]
    tile = 256
    whole = lambda i: (0, 0)
    step = lambda i: (i, 0)
    return pl.pallas_call(
        functools.partial(unproject_kernel, head_size),
        grid=(rows // tile,),
        in_specs=[
            pl.BlockSpec((tile, cols), step),
            pl.BlockSpec((tile, q_width), step),
            pl.BlockSpec((tile, cols - q_width), step),
            pl.BlockSpec((tile, LANES), step),
            pl.BlockSpec((tile, LANES), step),
            pl.BlockSpec((1, LANES), whole),
            pl.BlockSpec((1, LANES), whole),
        ],
        out_specs=[
            pl.BlockSpec((tile, cols), step),
            pl.BlockSpec((1, 2, LANES), lambda i: (i, 0, 0)),
        ],
        out_shape=[
            jax.ShapeDtypeStruct((rows, cols), BF),
            jax.ShapeDtypeStruct((rows // tile, 2, LANES), F32),
        ],
        compiler_params=pltpu.CompilerParams(vmem_limit_bytes=VMEM_LIMIT),
    )(raw, dq, dkv, cos, sin, query_gain, key_gain)


def unit_base(unit, places):
    los, span, block = places
    return (unit // los) * span + (unit % los) * block


def attend_kernel(
    head_size,
    places,
    code_ref,
    q_ref,
    kv_ref,
    row_ref,
    key_ref,
    exact_ref,
    low_ref,
    lse_ref,
    qs_ref,
    acc_ref,
    sum_ref,
):
    batch, part = pl.program_id(0), pl.program_id(2)
    count = row_ref.shape[1]
    share = kv_ref.shape[0]
    factor = LOG2E * head_size**-0.5
    lane = lane_index((count, LANES))

    @pl.when(part == 0)
    def _():
        both = q_ref[:, 0].reshape(count, LANES).astype(F32)
        qs_ref[0] = jnp.where(lane < head_size, both, 0.0).astype(BF)
        qs_ref[1] = jnp.where(lane < head_size, pltpu.roll(both, head_size, 1), 0.0).astype(BF)
        acc_ref[...] = jnp.zeros_like(acc_ref)
        sum_ref[...] = jnp.zeros_like(sum_ref)

    def one(at, masked):
        keys = kv_ref[at, :, 0].reshape(count, LANES)
        if masked:
            key_pos = key_ref[...] + unit_base(part * share + at, places)
            allowed = (key_pos <= row_ref[0, :, 0:1]) & (key_pos >= row_ref[0, :, 1:2])
        for head in range(2):
            exps = jnp.exp2(dot_back(qs_ref[head], keys) * factor)
            if masked:
                exps = jnp.where(allowed, exps, 0.0)
            partial = exps[:, :LANES]
            for lane_at in range(LANES, count, LANES):
                partial = partial + exps[:, lane_at : lane_at + LANES]
            sum_ref[head] += partial
            acc_ref[head] += dot_plain(exps.astype(BF), keys)

    def step(at, carry):
        code = code_ref[batch, part * share + at]

        @pl.when(code == 1)
        def _():
            one(at, False)

        @pl.when(code == 2)
        def _():
            one(at, True)

        return carry

    lax.fori_loop(0, share, step, 0)

    @pl.when(part == pl.num_programs(2) - 1)
    def _():
        results = []
        for head in range(2):
            total = jnp.sum(sum_ref[head], axis=-1, keepdims=True)
            results.append(acc_ref[head] / total)
            wide = jnp.broadcast_to(jnp.log2(total), (count, LANES))
            lse_ref[0, 0, head] = wide.T[:8]
        joined = jnp.where(lane < head_size, pltpu.roll(results[0], head_size, 1), results[1])
        joined = joined.reshape(exact_ref.shape[0], -1, LANES)
        exact_ref[:, 0] = joined
        low_ref[:, 0] = joined.astype(BF)


def attend(codes, query, kv_all, row_info, key_pos, places, head_size):
    slots, batches, rows, q_width = query.shape
    units = kv_all.shape[0]
    share = math.gcd(units, 8)
    count = slots * rows
    pairs = q_width // LANES
    pick = lambda b, p, u, codes: (0, b, 0, p)
    return pl.pallas_call(
        functools.partial(attend_kernel, head_size, places),
        grid_spec=pltpu.PrefetchScalarGridSpec(
            num_scalar_prefetch=1,
            grid=(batches, pairs, units // share),
            in_specs=[
                pl.BlockSpec((slots, 1, rows, LANES), pick),
                pl.BlockSpec(
                    (share, slots, 1, rows, LANES), lambda b, p, u, codes: (u, 0, b, 0, p)
                ),
                pl.BlockSpec((1, count, 2), lambda b, p, u, codes: (b, 0, 0)),
                pl.BlockSpec((1, count), lambda b, p, u, codes: (0, 0)),
            ],
            out_specs=[
                pl.BlockSpec((slots, 1, rows, LANES), pick),
                pl.BlockSpec((slots, 1, rows, LANES), pick),
                pl.BlockSpec((1, 1, 2, 8, count), lambda b, p, u, codes: (b, p, 0, 0, 0)),
            ],
            scratch_shapes=[
                pltpu.VMEM((2, count, LANES), BF),
                pltpu.VMEM((2, count, LANES), F32),
                pltpu.VMEM((2, count, LANES), F32),
            ],
        ),
        out_shape=[
            jax.ShapeDtypeStruct(query.shape, F32),
            jax.ShapeDtypeStruct(query.shape, BF),
            jax.ShapeDtypeStruct((batches, pairs, 2, 8, count), F32),
        ],
        compiler_params=pltpu.CompilerParams(vmem_limit_bytes=VMEM_LIMIT),
    )(codes, query, kv_all, row_info, key_pos)


def attend_back_kernel(
    head_size,
    places,
    code_ref,
    q_ref,
    up_ref,
    exact_ref,
    lse_ref,
    kv_ref,
    row_ref,
    key_ref,
    dq_ref,
    dkv_ref,
    qs_ref,
    us_ref,
    acc_ref,
    delta_ref,
):
    batch, part = pl.program_id(0), pl.program_id(2)
    count = row_ref.shape[2]
    share = kv_ref.shape[0]
    scale = head_size**-0.5
    factor = LOG2E * scale
    lane = lane_index((count, LANES))

    @pl.when(part == 0)
    def _():
        both = q_ref[:, 0].reshape(count, LANES).astype(F32)
        qs_ref[0] = jnp.where(lane < head_size, both, 0.0).astype(BF)
        qs_ref[1] = jnp.where(lane < head_size, pltpu.roll(both, head_size, 1), 0.0).astype(BF)
        upper = up_ref[:, 0].reshape(count, LANES).astype(F32)
        us_ref[0] = jnp.where(lane < head_size, 0.0, pltpu.roll(upper, head_size, 1)).astype(BF)
        us_ref[1] = jnp.where(lane < head_size, 0.0, upper).astype(BF)
        products = upper * exact_ref[:, 0].reshape(count, LANES)
        for head in range(2):
            inside = (lane < head_size) if head == 0 else (lane >= head_size)
            total = jnp.sum(jnp.where(inside, products, 0.0), axis=-1, keepdims=True)
            delta_ref[head] = jnp.broadcast_to(total, (count, LANES)).T[:8]
        acc_ref[...] = jnp.zeros_like(acc_ref)

    def one(at, masked):
        keys = kv_ref[at, :, 0].reshape(count, LANES)
        if masked:
            key_pos = key_ref[...] + unit_base(part * share + at, places)
            allowed = (key_pos <= row_ref[0, 0:1]) & (key_pos >= row_ref[0, 1:2])
        grad_kv = jnp.zeros((count, LANES), F32)
        for head in range(2):
            scores = dot_back(keys, qs_ref[head]) * factor
            probs = jnp.exp2(scores - lse_ref[0, 0, head, 0:1])
            if masked:
                probs = jnp.where(allowed, probs, 0.0)
            grads = dot_back(keys, us_ref[head])
            grads = (probs * (grads - delta_ref[head, 0:1])).astype(BF)
            grad_kv += dot_plain(probs.astype(BF), us_ref[head])
            grad_kv += dot_plain(grads, qs_ref[head]) * scale
            acc_ref[head] += dot_outer(grads, keys)
        dkv_ref[at, :, 0] = grad_kv.astype(BF).reshape(dkv_ref.shape[1], -1, LANES)

    def step(at, carry):
        code = code_ref[batch, part * share + at]

        @pl.when(code == 0)
        def _():
            dkv_ref[at, :, 0] = jnp.zeros((dkv_ref.shape[1],) + dkv_ref.shape[3:], BF)

        @pl.when(code == 1)
        def _():
            one(at, False)

        @pl.when(code == 2)
        def _():
            one(at, True)

        return carry

    lax.fori_loop(0, share, step, 0)

    @pl.when(part == pl.num_programs(2) - 1)
    def _():
        joined = jnp.where(lane < head_size, acc_ref[0], pltpu.roll(acc_ref[1], head_size, 1))
        dq_ref[:, 0] = (joined * scale).reshape(dq_ref.shape[0], -1, LANES)


def attend_back(codes, query, upstream, exact, lse, kv_all, row_info, key_pos, places, head_size):
    slots, batches, rows, q_width = query.shape
    units = kv_all.shape[0]
    share = math.gcd(units, 8)
    count = slots * rows
    pairs = q_width // LANES
    pick = lambda b, p, u, codes: (0, b, 0, p)
    pick_kv = lambda b, p, u, codes: (u, 0, b, 0, p)
    return pl.pallas_call(
        functools.partial(attend_back_kernel, head_size, places),
        grid_spec=pltpu.PrefetchScalarGridSpec(
            num_scalar_prefetch=1,
            grid=(batches, pairs, units // share),
            in_specs=[
                pl.BlockSpec((slots, 1, rows, LANES), pick),
                pl.BlockSpec((slots, 1, rows, LANES), pick),
                pl.BlockSpec((slots, 1, rows, LANES), pick),
                pl.BlockSpec((1, 1, 2, 8, count), lambda b, p, u, codes: (b, p, 0, 0, 0)),
                pl.BlockSpec((share, slots, 1, rows, LANES), pick_kv),
                pl.BlockSpec((1, 2, count), lambda b, p, u, codes: (b, 0, 0)),
                pl.BlockSpec((count, 1), lambda b, p, u, codes: (0, 0)),
            ],
            out_specs=[
                pl.BlockSpec((slots, 1, rows, LANES), pick),
                pl.BlockSpec((share, slots, 1, rows, LANES), pick_kv),
            ],
            scratch_shapes=[
                pltpu.VMEM((2, count, LANES), BF),
                pltpu.VMEM((2, count, LANES), BF),
                pltpu.VMEM((2, count, LANES), F32),
                pltpu.VMEM((2, 8, count), F32),
            ],
        ),
        out_shape=[
            jax.ShapeDtypeStruct(query.shape, F32),
            jax.ShapeDtypeStruct(kv_all.shape, BF),
        ],
        compiler_params=pltpu.CompilerParams(vmem_limit_bytes=VMEM_LIMIT),
    )(codes, query, upstream, exact, lse, kv_all, row_info, key_pos)


def per_device(
    inputs,
    cotangent,
    attn_gain,
    w_query,
    w_key,
    w_value,
    w_output,
    query_gain,
    key_gain,
    ffn_gain,
    w_gate,
    w_up,
    w_down,
    doc_starts,
):
    heads, mids = lax.axis_size("heads"), lax.axis_size("mid")
    his, los = lax.axis_size("hi"), lax.axis_size("lo")
    slots, units = heads * mids, his * los
    batches, _, rows, width = inputs.shape
    block = rows * heads
    count = slots * rows
    head_size = query_gain.shape[0]
    w_rows = w_query.shape[0]
    q_width = w_query.shape[1] // slots
    pairs = w_key.shape[1] // head_size // slots
    ff_width = w_gate.shape[1] // slots

    by_slot = lambda w: w.reshape(w_rows, slots, -1)
    kv_cols = jnp.stack(
        [
            w_key.reshape(w_rows, slots, pairs, head_size),
            w_value.reshape(w_rows, slots, pairs, head_size),
        ],
        axis=3,
    )
    qkv_part = columns_out(
        jnp.concatenate([by_slot(w_query), kv_cols.reshape(w_rows, slots, -1)], axis=2)
    )
    w_qkv = natural_rows(gather_data(qkv_part))
    own_in = inputs[:, 0]
    in_all = group_gather(own_in)
    own_cot = cotangent[:, 0]
    cot_all = group_gather(own_cot)
    wo_part = rows_out(w_output)
    gate_up_part = columns_out(jnp.concatenate([by_slot(w_gate), by_slot(w_up)], axis=2))
    wd_part = rows_out(w_down)

    head_at, mid_at = slot_places()
    row_at = jnp.arange(rows, dtype=jnp.int32)
    hi_at, lo_at = lax.axis_index("hi"), lax.axis_index("lo")

    def positions(hi, lo):
        blocks = (hi * mids + mid_at) * los + lo
        return (blocks * block + head_at * rows)[:, None] + row_at[None, :]

    row_pos = positions(hi_at, lo_at).reshape(count)
    first_pos = positions(0, 0).reshape(count)
    places = (los, mids * los * block, block)
    unit_at = unit_base(jnp.arange(units, dtype=jnp.int32), places)
    starts = doc_starts[:, None, :]
    row_begin = jnp.max(jnp.where(starts <= row_pos[None, :, None], starts, 0), axis=2)
    row_both = jnp.broadcast_to(row_pos[None], (batches, count))
    key_low, key_high = (unit_at + jnp.min(first_pos))[None], (unit_at + jnp.max(first_pos))[None]
    begin_low, begin_high = (
        jnp.min(row_begin, axis=1)[:, None],
        jnp.max(row_begin, axis=1)[:, None],
    )
    none = (key_low > jnp.max(row_pos)) | (key_high < begin_low)
    full = (key_high <= jnp.min(row_pos)) & (key_low >= begin_high)
    codes = jnp.where(none, 0, jnp.where(full, 1, 2)).astype(jnp.int32)
    info_cols = jnp.stack([row_both, row_begin], axis=2)
    info_rows = jnp.stack([row_both, row_begin], axis=1)

    half = head_size // 2
    frequency = THETA ** (-(jnp.arange(half, dtype=F32) * 2.0 / head_size))
    turn_pos = (row_both - row_begin).reshape(batches, slots, rows).transpose(1, 0, 2)
    angles = turn_pos.reshape(-1).astype(F32)[:, None] * frequency[None, :]
    cos, sin = jnp.cos(angles), jnp.sin(angles)
    cos = jnp.concatenate([cos] * 4, axis=1)
    sin = jnp.concatenate([-sin, sin, -sin, sin], axis=1)
    q_gain = jnp.concatenate([query_gain, query_gain])[None]
    k_gain = jnp.concatenate([key_gain, key_gain])[None]

    in_wide = in_all.reshape(-1, width).astype(F32)
    in_unit = in_wide * rms_inverse(in_wide)
    normed = (in_unit * attn_gain).astype(BF)
    raw, query, kv = project(normed, w_qkv, cos, sin, q_gain, k_gain, q_width, head_size)
    query = query.reshape(slots, batches, rows, q_width)
    kv_all = gather_data(kv.reshape(slots, batches, rows, -1))
    wo_use = gather_data(wo_part).reshape(-1, width)
    w_gate_up = natural_rows(gather_data(gate_up_part))
    wg_use, wu_use = w_gate_up[:, :ff_width], w_gate_up[:, ff_width:]
    wd_use = gather_data(wd_part).reshape(-1, width)
    exact, attn, lse = attend(
        codes, query, kv_all, info_cols, first_pos[None], places, head_size
    )
    attn = attn.reshape(-1, q_width)
    by_slots = lambda total: total.astype(BF).reshape(slots, batches * rows, width)
    middle = own_in.reshape(-1, width).astype(F32) + group_sum(by_slots(dot_plain(attn, wo_use)))

    normed_two = (middle * rms_inverse(middle) * ffn_gain).astype(BF)
    normed_two_all = group_gather(normed_two).reshape(-1, width)
    cot_rows = cot_all.reshape(-1, width)
    gate = dot_plain(normed_two_all, wg_use)
    upper = dot_plain(normed_two_all, wu_use)
    grad_hidden = dot_back(cot_rows, wd_use)
    sigmoid = jax.nn.sigmoid(gate)
    silu = gate * sigmoid
    hidden = (silu * upper).astype(BF)
    grad_gate = (grad_hidden * upper * sigmoid * (1.0 + gate * (1.0 - sigmoid))).astype(BF)
    grad_upper = (grad_hidden * silu).astype(BF)
    grad_two = group_sum(by_slots(dot_back(grad_gate, wg_use) + dot_back(grad_upper, wu_use)))
    grad_gate_up = jnp.concatenate(
        [dot_outer(normed_two_all, grad_gate), dot_outer(normed_two_all, grad_upper)], axis=1
    )
    gate_up_sum = scatter_rows(grad_gate_up.astype(BF))
    down_sum = lax.psum_scatter(
        dot_outer(hidden, cot_rows).astype(BF), DATA, scatter_dimension=0, tiled=True
    )
    block_out = (middle + group_sum(by_slots(dot_plain(hidden, wd_use)))).astype(BF)
    grad_mid_part, ffn_gain_part = norm_back(middle, ffn_gain, grad_two)
    grad_middle = own_cot.reshape(-1, width).astype(F32) + grad_mid_part

    grad_mid_all = group_gather(grad_middle.astype(BF)).reshape(-1, width)
    grad_attn = dot_back(grad_mid_all, wo_use).astype(BF).reshape(query.shape)
    dq, dkv = attend_back(
        codes,
        query,
        grad_attn,
        exact,
        lse,
        kv_all,
        info_rows,
        first_pos[:, None],
        places,
        head_size,
    )
    dkv_mine = lax.psum_scatter(dkv, DATA, scatter_dimension=0, tiled=False)
    grad_output = dot_outer(attn, grad_mid_all)
    output_sum = lax.psum_scatter(grad_output.astype(BF), DATA, scatter_dimension=0, tiled=True)
    grad_raw, head_gains = unproject(
        raw,
        dq.reshape(-1, q_width),
        dkv_mine.reshape(raw.shape[0], -1),
        cos,
        sin,
        q_gain,
        k_gain,
        head_size,
    )
    grad_normed_low = dot_back(grad_raw, w_qkv).astype(BF)
    grad_qkv = dot_outer(normed, grad_raw)
    qkv_sum = scatter_rows(grad_qkv.astype(BF))
    grad_normed = group_sum(grad_normed_low.reshape(slots, batches * rows, width))
    grad_in_part, _ = norm_back(own_in.reshape(-1, width).astype(F32), attn_gain, grad_normed)
    grad_inputs = grad_middle + grad_in_part
    attn_gain_part = jnp.sum(grad_normed_low.astype(F32) * in_unit, axis=0)

    qkv_cols = columns_out(qkv_sum.transpose(1, 0, 2)).transpose(1, 0, 2).astype(F32)
    gate_up_cols = columns_out(gate_up_sum.transpose(1, 0, 2)).transpose(1, 0, 2).astype(F32)
    kv_sums = qkv_cols[:, :, q_width:].reshape(w_rows, slots, pairs, 2, head_size)
    head_sums = jnp.sum(head_gains, axis=0).reshape(2, 2, head_size).sum(axis=1)
    gains = all_sum(
        jnp.concatenate(
            [attn_gain_part, jnp.sum(ffn_gain_part, axis=0), head_sums[0], head_sums[1]]
        )
    )
    return (
        block_out.reshape(batches, 1, rows, width),
        grad_inputs.reshape(batches, 1, rows, width),
        gains[:width],
        qkv_cols[:, :, :q_width].reshape(w_rows, -1),
        kv_sums[:, :, :, 0].reshape(w_rows, -1),
        kv_sums[:, :, :, 1].reshape(w_rows, -1),
        rows_back(output_sum).astype(F32),
        gains[2 * width : 2 * width + head_size],
        gains[2 * width + head_size :],
        gains[width : 2 * width],
        gate_up_cols[:, :, :ff_width].reshape(w_rows, -1),
        gate_up_cols[:, :, ff_width:].reshape(w_rows, -1),
        rows_back(down_sum).astype(F32),
    )


def solution(mesh):
    heads, seq = mesh.shape["heads"], mesh.shape["seq"]
    rows_spec = P(None, SEQ, "heads", None)
    weight_spec = P(ALL, None)

    def run(*args):
        kv_heads = args[4].shape[1] // args[7].shape[0]
        low = 2 if seq % 2 == 0 else 1
        mid = 2 if seq % (2 * low) == 0 and kv_heads % (2 * heads) == 0 else 1
        split = Mesh(
            mesh.devices.reshape(heads, seq // (mid * low), mid, low), ("heads",) + SEQ
        )
        return jax.shard_map(
            per_device,
            mesh=split,
            in_specs=(
                (rows_spec, rows_spec, P())
                + (weight_spec,) * 4
                + (P(), P(), P())
                + (weight_spec,) * 3
                + (P(),)
            ),
            out_specs=(
                (rows_spec, rows_spec, P())
                + (weight_spec,) * 4
                + (P(), P(), P())
                + (weight_spec,) * 3
            ),
            check_vma=False,
        )(*args)

    return run
```

time: 1640 us -> 533 us (0.33)
  waiting for transfers between devices: 605 us -> 223 us
  blocking collectives: 343 us -> 49.7 us
  matrix products: 343 us -> 53.2 us
  local copies, waits for them, and re-layouts: 158 us -> 38.4 us
  other arithmetic: 134 us -> 34.3 us
  Pallas kernels: 0 us -> 44.7 us
  starting transfers between devices: 25.2 us -> 66.2 us
    reduce_scatter x19 -> x5, waiting for transfers between devices: 490 us -> 115 us  [the longest x1 50.7 us: per_device(): dkv_mine = lax.psum_scatter(dkv, DATA, scatter_dimension=0, tiled=False)]
    dot_general x126 -> x4, matrix products: 283 us -> 13.9 us  [dot_plain(): return jnp.dot(left_side, right_side, preferred_element_type=F32)]
    all_gather x10 -> x1, blocking collectives: 163 us -> 20.5 us  [gather_data(): return lax.all_gather(part, DATA, axis=0, tiled=False)]
    all_to_all x5 -> x1, blocking collectives: 139 us -> 29.2 us  [columns_out(): lax.all_to_all(parts.transpose(1, 0, 2), GROUP, split_axis=0, concat_axis...]
    ppermute x0 -> x41, waiting for transfers between devices: none -> 70.3 us  [the longest x32 66.6 us: swap(): return lax.ppermute(part, axis, [(0, 1), (1, 0)])]
    all_to_all x5 -> x3, waiting for transfers between devices: 75.4 us -> 7.53 us  [columns_out(): lax.all_to_all(parts.transpose(1, 0, 2), GROUP, split_axis=0, concat_axis...]
    reduce_sum x21 -> x6, other arithmetic: 59.9 us -> 3.56 us  [the longest x3 2.1 us: rms_inverse(): return lax.rsqrt(jnp.mean(values * values, axis=-1, keepdims=True) + EPS)]
    ppermute x0 -> x41, starting transfers between devices: none -> 55.1 us  [the longest x32 39.9 us: swap(): return lax.ppermute(part, axis, [(0, 1), (1, 0)])]
  transfers between devices with their start and end apart: 33 -> 53, of which waited for: 14 -> 31; matrix products, arithmetic and copies ran while one was open for 30% -> 17% of each run, Pallas kernels for 0% -> 7%
where the time goes in v1:
time: 533 us; the launch traced here: 525 us
  waiting for transfers between devices  223 us (42%)
  starting transfers between devices  66.2 us (12%)
  matrix products  53.2 us (10%)
  blocking collectives  49.7 us (9%)
  Pallas kernels  44.7 us (8%)
  local copies, waits for them, and re-layouts  38.4 us (7%)
  other arithmetic  34.3 us (6%)
  between operations  15.1 us (3%)
    ppermute x32, waiting for transfers between devices, swap(): return lax.ppermute(part, axis, [(0, 1), (1, 0)])  66.6 us
    reduce_scatter x1, waiting for transfers between devices, per_device(): dkv_mine = lax.psum_scatter(dkv, DATA, scatter_dimension=0, tiled=False)  50.7 us
    reduce_scatter x2, waiting for transfers between devices, scatter_rows(): lax.psum_scatter(parts.reshape(his * los, heads * mids * rows, cols), DAT...  48.4 us
    ppermute x32, starting transfers between devices, swap(): return lax.ppermute(part, axis, [(0, 1), (1, 0)])  39.9 us
    all_gather x4, waiting for transfers between devices, gather_data(): return lax.all_gather(part, DATA, axis=0, tiled=False)  29.9 us
    all_to_all x1, blocking collectives, columns_out(): lax.all_to_all(parts.transpose(1, 0, 2), GROUP, split_axis=0, concat_axis...  29.2 us
    pallas_call x1, Pallas kernels, attend_back(): pl.pallas_call(functools.partial(attend_back_kernel, head_size, places),...  21.4 us
    all_gather x1, blocking collectives, gather_data(): return lax.all_gather(part, DATA, axis=0, tiled=False)  20.5 us
  transfers between devices with their start and end apart: 53, of which 31 were waited for; matrix products, arithmetic and copies ran while one was open for 17% of the time, Pallas kernels for 7%

profile of v1, /device:TPU:0, one launch (start us, length us, event | category | flops | bytes accessed | tf_op | source)
XLA Modules:
  0.0 525.0 jit_solution(1387036465489018413)
XLA Ops:
  7.2 3.0 collective-permute-start
  15.9 3.3 all-to-all-start
  20.2 5.0 all-to-all-done
  35.2 3.2 multiply_convert_fusion.3.normed_ref
  38.4 10.1 %all-gather.11.cloned.1.call-done = bf16[32,32,512]{2,1,0:T(8,128)(2,1)} async-done(((bf16[4,32,512]{2,1,0:T(8,128)(2,1)}), bf16[32,32,512]{2,1,0:T(8,128)(2,1)}) %all-gather.11.cloned.1.call-update) | async-done | bytes 1048592 | tf_op jit(solution)/shard_map/all_gather | solution.py:121
  49.8 6.1 %shard_map.237 = (f32[1024,512]{1,0:T(8,128)S(1)}, bf16[1024,256]{1,0:T(8,128)(2,1)S(1)}, bf16[1024,256]{1,0:T(8,128)(2,1)}) custom-call(bf16[1024,1024]{1,0:T(8,128)(2,1)} %multiply_convert_fusion.3.normed_ref, bf16[1024,512]{1,0:T(8,128)(2,1)S(1)} %bitcast.245, f32[1024,128]{1,0:T(8,128)S(1)} %get-tuple-element.231.cos_ref, ...), custom_call_target="tpu_custom_call" | custom-call | tf_op jit(solution)/shard_map/pallas_call | solution.py:212
  61.1 29.2 %all_to_all.20 = bf16[4,32,2304]{2,1,0:T(8,128)(2,1)} all-to-all(bf16[4,32,2304]{2,1,0:T(8,128)(2,1)S(1)} %copy.194), channel_id=1, replica_groups=mesh['heads'=2,'hi'=4,'mid'=2,'lo'=2] {'heads','mid'}, dimensions={0} | all-to-all | bytes 1179648 | tf_op jit(solution)/shard_map/all_to_all | solution.py:115
  94.6 2.6 broadcast_compare_fusion
  97.6 20.5 %all-gather.1 = bf16[256,1024]{1,0:T(8,128)(2,1)} all-gather(bf16[32,1024]{1,0:T(8,128)(2,1)S(1)} %collective-permute-done.4), channel_id=3, replica_groups=mesh['heads'=2,'hi'=4,'mid'=2,'lo'=2] {'hi','lo'}, dimensions={0}, use_global_device_ids=true | all-gather | bytes 589824 | tf_op jit(solution)/shard_map/all_gather | solution.py:121
  119.2 13.3 %shard_map.238 = (f32[4,2,128,256]{3,2,1,0:T(8,128)S(1)}, bf16[4,2,128,256]{3,2,1,0:T(8,128)(2,1)S(1)}, f32[2,2,2,8,512]{4,3,2,1,0:T(8,128)S(1)}) custom-call(s32[2,8]{1,0:T(2,128)S(1)} %or_select_fusion.code_ref, bf16[4,2,128,256]{3,2,1,0:T(8,128)(2,1)S(1)} %bitcast.249, bf16[8,4,2,128,256]{4,3,2,1,0:T(8,128)(2,1)} %all-gather.9.cloned.1.call-done.kv_ref, ...), custom_call_target="tpu_custom_call" | custom-call | tf_op jit(solution)/shard_map/pallas_call | solution.py:382
  139.9 2.7 collective-permute-done.5
  150.0 3.1 pad_maximum_fusion.2
  153.1 7.5 %collective-permute-done.6 = bf16[256,1024]{1,0:T(8,128)(2,1)S(1)} collective-permute-done((bf16[256,1024]{1,0:T(8,128)(2,1)S(1)}, bf16[256,1024]{1,0:T(8,128)(2,1)S(1)}, u32[]{:S(2)}, u32[]{:S(2)}) %collective-permute-start.6) | collective-permute-done | bytes 524320 | tf_op jit(solution)/shard_map/ppermute | solution.py:57
  165.2 7.5 %fusion.45 = f32[1024,1152]{1,0:T(8,128)} fusion(bf16[1024,1024]{1,0:T(8,128)(2,1)} %bitcast.285, bf16[1152,1024]{1,0:T(8,128)(2,1)} %all-gather.15.cloned.1.call-done), kind=kOutput, calls=%fused_computation.165 | convolution fusion | flops 2415919104 | bytes 9175040 | tf_op jit(solution)/shard_map/dot_general | solution.py:29
  172.7 19.9 %all-gather.13.cloned.1.call-done = bf16[32,32,2304]{2,1,0:T(8,128)(2,1)} async-done(((bf16[4,32,2304]{2,1,0:T(8,128)(2,1)}), bf16[32,32,2304]{2,1,0:T(8,128)(2,1)}) %all-gather.13.cloned.1.call-update) | async-done | bytes 4718608 | tf_op jit(solution)/shard_map/all_gather | solution.py:121
  192.6 2.8 copy.195
  199.7 4.3 collective-permute-done.11
  207.6 2.9 fusion.5
  210.6 7.2 %multiply_convert_fusion.1 = (bf16[1024,1152]{1,0:T(8,128)(2,1)}, bf16[1024,1152]{1,0:T(8,128)(2,1)S(1)}, bf16[1024,1152]{1,0:T(8,128)(2,1)S(1)}) fusion(f32[1024,1152]{1,0:T(8,128)S(1)} %bitcast.309, f32[1024,1152]{1,0:T(8,128)S(1)} %fusion.5, bf16[1024,1024]{1,0:T(8,128)(2,1)S(1)} %bitcast.265, bf16[1024,2304]{1,0:T(8,128)(2,1)S(1)} %bitcast.271), kind=kOutput, calls=%fused_computation.2 | convolution fusion | flops 2433613824 | bytes 20971520 | tf_op jit(solution)/shard_map/dot_general | solution.py:25
  217.8 2.9 fusion.3
  221.2 3.1 add_convert_fusion
  226.5 3.1 convolution_convert_fusion.3
  232.8 2.4 collective-permute-start.23
  242.7 8.9 %collective-permute-done.23 = bf16[256,1024]{1,0:T(8,128)(2,1)S(1)} collective-permute-done((bf16[256,1024]{1,0:T(8,128)(2,1)S(1)}, bf16[256,1024]{1,0:T(8,128)(2,1)S(1)}, u32[]{:S(2)}, u32[]{:S(2)}) %collective-permute-start.23) | collective-permute-done | bytes 524320 | tf_op jit(solution)/shard_map/ppermute | solution.py:57
  252.8 7.3 %collective-permute-done.15 = bf16[256,1024]{1,0:T(8,128)(2,1)S(1)} collective-permute-done((bf16[256,1024]{1,0:T(8,128)(2,1)S(1)}, bf16[256,1024]{1,0:T(8,128)(2,1)S(1)}, u32[]{:S(2)}, u32[]{:S(2)}) %collective-permute-start.15) | collective-permute-done | bytes 524320 | tf_op jit(solution)/shard_map/ppermute | solution.py:57
  260.2 3.0 fusion.40
  266.0 9.1 %collective-permute-done.26 = bf16[256,1024]{1,0:T(8,128)(2,1)S(1)} collective-permute-done((bf16[256,1024]{1,0:T(8,128)(2,1)S(1)}, bf16[256,1024]{1,0:T(8,128)(2,1)S(1)}, u32[]{:S(2)}, u32[]{:S(2)}) %collective-permute-start.26) | collective-permute-done | bytes 524320 | tf_op jit(solution)/shard_map/ppermute | solution.py:57
  278.4 3.5 collective-permute-done.28
  287.2 6.3 %convolution_convert_fusion = bf16[1152,1024]{1,0:T(8,128)(2,1)} fusion(bf16[1024,1152]{1,0:T(8,128)(2,1)} %copy-done.43, bf16[1024,1024]{1,0:T(8,128)(2,1)} %bitcast.286), kind=kOutput, calls=%fused_computation.11 | convolution fusion | flops 2417098752 | bytes 6815744 | tf_op jit(solution)/shard_map/dot_general | solution.py:35
  294.6 2.5 convolution_convert_fusion.8
  297.1 21.4 %shard_map.239 = (f32[4,2,128,256]{3,2,1,0:T(8,128)S(1)}, bf16[8,4,2,128,256]{4,3,2,1,0:T(8,128)(2,1)}) custom-call(s32[2,8]{1,0:T(2,128)S(1)} %or_select_fusion.code_ref, bf16[4,2,128,256]{3,2,1,0:T(8,128)(2,1)S(1)} %bitcast.250, bf16[4,2,128,256]{3,2,1,0:T(8,128)(2,1)S(1)} %bitcast.253, f32[4,2,128,256]{3,2,1,0:T(8,128)S(1)} %copy-done.6, ...), custom_call_target="tpu_custom_call" | custom-call | tf_op jit(solution)/shard_map/pallas_call | solution.py:506
  318.5 3.9 copy.201
  322.5 5.4 %convolution_convert_fusion.1 = bf16[2,4,2,2,32,1152]{5,4,3,2,1,0:T(8,128)(2,1)S(1)} fusion(bf16[2,4,2,2,32,1024]{5,4,3,2,1,0:T(8,128)(2,1)} %bitcast.287, bf16[1024,1152]{1,0:T(8,128)(2,1)} %copy-done.42), kind=kOutput, calls=%fused_computation.12 | convolution fusion | flops 2417098752 | bytes 6815744 | tf_op jit(solution)/shard_map/dot_general | solution.py:35
  327.8 3.1 convolution_convert_fusion.2
  331.5 2.6 copy.202
  336.9 16.2 %reduce-scatter.14.cloned.1.call-done = bf16[144,1024]{1,0:T(8,128)(2,1)} async-done(((bf16[1152,1024]{1,0:T(8,128)(2,1)}), bf16[144,1024]{1,0:T(8,128)(2,1)}) %reduce-scatter.14.cloned.1.call-update) | async-done | bytes 294928 | tf_op jit(solution)/shard_map/reduce_scatter | solution.py:656
  353.1 3.7 collective-permute-start.40
  356.9 50.7 %reduce-scatter.6.cloned.1.call-done = bf16[1,4,2,128,256]{4,3,2,1,0:T(8,128)(2,1)} async-done(((bf16[8,4,2,128,256]{4,3,2,1,0:T(8,128)(2,1)}), bf16[1,4,2,128,256]{4,3,2,1,0:T(8,128)(2,1)}) %reduce-scatter.6.cloned.1.call-update) | async-done | bytes 524304 | tf_op jit(solution)/shard_map/reduce_scatter | solution.py:677
  410.2 3.9 shard_map.240
  415.3 4.3 multiply_reduce_fusion
  422.2 44.7 %reduce-scatter.12.cloned.1.call-done = bf16[1,128,2304]{2,1,0:T(8,128)(2,1)} async-done(((bf16[8,128,2304]{2,1,0:T(8,128)(2,1)}), bf16[1,128,2304]{2,1,0:T(8,128)(2,1)}) %reduce-scatter.12.cloned.1.call-update) | async-done | bytes 589840 | tf_op jit(solution)/shard_map/reduce_scatter | solution.py:138
  466.9 3.7 all-to-all-start.3
  472.9 2.9 convolution_convert_fusion.6
  495.0 5.3 %collective-permute-done.31 = bf16[256,1024]{1,0:T(8,128)(2,1)S(1)} collective-permute-done((bf16[256,1024]{1,0:T(8,128)(2,1)S(1)}, bf16[256,1024]{1,0:T(8,128)(2,1)S(1)}, u32[]{:S(2)}, u32[]{:S(2)}) %collective-permute-start.31) | collective-permute-done | bytes 524320 | tf_op jit(solution)/shard_map/ppermute | solution.py:57
  503.1 3.7 reduce-scatter.8.cloned.1.call-done
  506.8 3.7 all-to-all-start.2
  510.4 2.5 fusion.18
  513.0 2.5 all-to-all-done.2
  (299 shorter events, 119.3 us)
Async XLA Ops:
  7.2 19.1 %collective-permute-start = (bf16[2,128,1024]{2,1,0:T(8,128)(2,1)}, bf16[2,128,1024]{2,1,0:T(8,128)(2,1)S(1)}, u32[]{:S(2)}, u32[]{:S(2)}) collective-permute-start(bf16[2,128,1024]{2,1,0:T(8,128)(2,1)} %bitcast.257), channel_id=1, source_target_pairs={{0,2},{2,0},{1,3},{3,1},{4,6},{6,4},{5,7},{7,5},{8,10},{10,8},{9,1... | collective-permute-start | bytes 1572872 | tf_op jit(solution)/shard_map/ppermute | solution.py:57
  10.2 17.7 %collective-permute-start.1 = (bf16[2,128,1024]{2,1,0:T(8,128)(2,1)}, bf16[2,128,1024]{2,1,0:T(8,128)(2,1)S(1)}, u32[]{:S(2)}, u32[]{:S(2)}) collective-permute-start(bf16[2,128,1024]{2,1,0:T(8,128)(2,1)} %bitcast.258), channel_id=1, source_target_pairs={{0,16},{16,0},{1,17},{17,1},{2,18},{18,2},{3,19},{19,3},{4,20},{20... | collective-permute-start | bytes 1572872 | tf_op jit(solution)/shard_map/ppermute | solution.py:57
  15.9 9.3 %all-to-all-start = ((bf16[4,32,512]{2,1,0:T(8,128)(2,1)}), bf16[4,32,512]{2,1,0:T(8,128)(2,1)S(1)}, u32[]{:S(2)}, u32[]{:S(2)}) async-start(bf16[4,32,512]{2,1,0:T(8,128)(2,1)} %copy.189), calls=%async_computation | async-start | bytes 262144 | tf_op jit(solution)/shard_map/all_to_all | solution.py:115
  19.2 29.2 %all-gather.11.cloned.1.call-start = ((), (), s32[]{:S(2)}) async-start(), calls=%async_computation.15 | async-start | bytes 1179648 | tf_op jit(solution)/shard_map/all_gather | solution.py:121
  25.9 92.3 %all-gather.9.cloned.1.call-start = ((), (), s32[]{:S(2)}) async-start(), calls=%async_computation.9 | async-start | bytes 4718592 | tf_op jit(solution)/shard_map/all_gather | solution.py:121
  26.3 6.7 %collective-permute-start.2 = (bf16[1,128,1024]{2,1,0:T(8,128)(2,1)S(1)}, bf16[1,128,1024]{2,1,0:T(8,128)(2,1)S(1)}, u32[]{:S(2)}, u32[]{:S(2)}) collective-permute-start(bf16[1,128,1024]{2,1,0:T(8,128)(2,1)S(1)} %slice.204), channel_id=1, source_target_pairs={{0,16},{16,0},{1,17},{17,1},{2,18},{18,2},{3,19},{19,3},{4,20},{20... | collective-permute-start | bytes 786440 | tf_op jit(solution)/shard_map/ppermute | solution.py:57
  27.9 6.6 %collective-permute-start.3 = (bf16[1,128,1024]{2,1,0:T(8,128)(2,1)S(1)}, bf16[1,128,1024]{2,1,0:T(8,128)(2,1)S(1)}, u32[]{:S(2)}, u32[]{:S(2)}) collective-permute-start(bf16[1,128,1024]{2,1,0:T(8,128)(2,1)S(1)} %slice.205), channel_id=1, source_target_pairs={{0,2},{2,0},{1,3},{3,1},{4,6},{6,4},{5,7},{7,5},{8,10},{10,8},{9,1... | collective-permute-start | bytes 786440 | tf_op jit(solution)/shard_map/ppermute | solution.py:57
  58.1 107.1 %all-gather.15.cloned.1.call-start = ((), (), s32[]{:S(2)}) async-start(), calls=%async_computation.17 | async-start | bytes 2654208 | tf_op jit(solution)/shard_map/all_gather | solution.py:121
  60.5 132.0 %all-gather.13.cloned.1.call-start = ((), (), s32[]{:S(2)}) async-start(), calls=%async_computation.16 | async-start | bytes 5308416 | tf_op jit(solution)/shard_map/all_gather | solution.py:121
  90.3 245.1 %reduce-scatter.10.cloned.1.call-start = ((), (), s32[]{:S(2)}) async-start(), calls=%async_computation.12 | async-start | bytes 589824 | tf_op jit(solution)/shard_map/reduce_scatter | solution.py:679
  90.4 46.9 %collective-permute-start.18 = (bf16[2,128,1024]{2,1,0:T(8,128)(2,1)}, bf16[2,128,1024]{2,1,0:T(8,128)(2,1)}, u32[]{:S(2)}, u32[]{:S(2)}) collective-permute-start(bf16[2,128,1024]{2,1,0:T(8,128)(2,1)} %bitcast.54), channel_id=1, source_target_pairs={{0,2},{2,0},{1,3},{3,1},{4,6},{6,4},{5,7},{7,5},{8,10},{10,8},{9,1... | collective-permute-start | bytes 1572872 | tf_op jit(solution)/shard_map/ppermute | solution.py:57
  91.3 47.5 %collective-permute-start.19 = (bf16[2,128,1024]{2,1,0:T(8,128)(2,1)}, bf16[2,128,1024]{2,1,0:T(8,128)(2,1)}, u32[]{:S(2)}, u32[]{:S(2)}) collective-permute-start(bf16[2,128,1024]{2,1,0:T(8,128)(2,1)} %bitcast.54), channel_id=1, source_target_pairs={{0,16},{16,0},{1,17},{17,1},{2,18},{18,2},{3,19},{19,3},{4,20},{20... | collective-permute-start | bytes 1572872 | tf_op jit(solution)/shard_map/ppermute | solution.py:57
  133.5 9.1 %collective-permute-start.5 = (bf16[128,1024]{1,0:T(8,128)(2,1)S(1)}, bf16[128,1024]{1,0:T(8,128)(2,1)S(1)}, u32[]{:S(2)}, u32[]{:S(2)}) collective-permute-start(bf16[128,1024]{1,0:T(8,128)(2,1)S(1)} %get-tuple-element.201), channel_id=1, source_target_pairs={{0,16},{16,0},{1,17},{17,1},{2,18},{18,2},{3,19},{19,3},{4,20},{20... | collective-permute-start | bytes 786440 | tf_op jit(solution)/shard_map/ppermute | solution.py:57
  135.1 9.3 %collective-permute-start.7 = (bf16[128,1024]{1,0:T(8,128)(2,1)S(1)}, bf16[128,1024]{1,0:T(8,128)(2,1)S(1)}, u32[]{:S(2)}, u32[]{:S(2)}) collective-permute-start(bf16[128,1024]{1,0:T(8,128)(2,1)S(1)} %get-tuple-element.200), channel_id=1, source_target_pairs={{0,2},{2,0},{1,3},{3,1},{4,6},{6,4},{5,7},{7,5},{8,10},{10,8},{9,1... | collective-permute-start | bytes 786440 | tf_op jit(solution)/shard_map/ppermute | solution.py:57
  138.2 9.6 %collective-permute-start.20 = (bf16[1,128,1024]{2,1,0:T(8,128)(2,1)S(1)}, bf16[1,128,1024]{2,1,0:T(8,128)(2,1)S(1)}, u32[]{:S(2)}, u32[]{:S(2)}) collective-permute-start(bf16[1,128,1024]{2,1,0:T(8,128)(2,1)S(1)} %slice.224), channel_id=1, source_target_pairs={{0,16},{16,0},{1,17},{17,1},{2,18},{18,2},{3,19},{19,3},{4,20},{20... | collective-permute-start | bytes 786440 | tf_op jit(solution)/shard_map/ppermute | solution.py:57
  139.8 10.1 %collective-permute-start.21 = (bf16[1,128,1024]{2,1,0:T(8,128)(2,1)S(1)}, bf16[1,128,1024]{2,1,0:T(8,128)(2,1)S(1)}, u32[]{:S(2)}, u32[]{:S(2)}) collective-permute-start(bf16[1,128,1024]{2,1,0:T(8,128)(2,1)S(1)} %slice.225), channel_id=1, source_target_pairs={{0,2},{2,0},{1,3},{3,1},{4,6},{6,4},{5,7},{7,5},{8,10},{10,8},{9,1... | collective-permute-start | bytes 786440 | tf_op jit(solution)/shard_map/ppermute | solution.py:57
  144.6 16.0 %collective-permute-start.6 = (bf16[256,1024]{1,0:T(8,128)(2,1)S(1)}, bf16[256,1024]{1,0:T(8,128)(2,1)S(1)}, u32[]{:S(2)}, u32[]{:S(2)}) collective-permute-start(bf16[256,1024]{1,0:T(8,128)(2,1)S(1)} %pad_maximum_fusion.6), channel_id=1, source_target_pairs={{0,2},{2,0},{1,3},{3,1},{4,6},{6,4},{5,7},{7,5},{8,10},{10,8},{9,1... | collective-permute-start | bytes 1572872 | tf_op jit(solution)/shard_map/ppermute | solution.py:57
  146.7 13.9 %collective-permute-start.8 = (bf16[256,1024]{1,0:T(8,128)(2,1)S(1)}, bf16[256,1024]{1,0:T(8,128)(2,1)S(1)}, u32[]{:S(2)}, u32[]{:S(2)}) collective-permute-start(bf16[256,1024]{1,0:T(8,128)(2,1)S(1)} %pad_maximum_fusion.7), channel_id=1, source_target_pairs={{0,16},{16,0},{1,17},{17,1},{2,18},{18,2},{3,19},{19,3},{4,20},{20... | collective-permute-start | bytes 1572872 | tf_op jit(solution)/shard_map/ppermute | solution.py:57
  162.9 32.5 %collective-permute-start.9 = (bf16[256,1024]{1,0:T(8,128)(2,1)}, bf16[256,1024]{1,0:T(8,128)(2,1)S(1)}, u32[]{:S(2)}, u32[]{:S(2)}) collective-permute-start(bf16[256,1024]{1,0:T(8,128)(2,1)} %multiply_convert_fusion.4), channel_id=1, source_target_pairs={{0,2},{2,0},{1,3},{3,1},{4,6},{6,4},{5,7},{7,5},{8,10},{10,8},{9,1... | collective-permute-start | bytes 1572872 | tf_op jit(solution)/shard_map/ppermute | solution.py:57
  164.7 32.3 %collective-permute-start.10 = (bf16[256,1024]{1,0:T(8,128)(2,1)}, bf16[256,1024]{1,0:T(8,128)(2,1)}, u32[]{:S(2)}, u32[]{:S(2)}) collective-permute-start(bf16[256,1024]{1,0:T(8,128)(2,1)} %multiply_convert_fusion.4), channel_id=1, source_target_pairs={{0,16},{16,0},{1,17},{17,1},{2,18},{18,2},{3,19},{19,3},{4,20},{20... | collective-permute-start | bytes 1572872 | tf_op jit(solution)/shard_map/ppermute | solution.py:57
  195.4 8.5 %collective-permute-start.11 = (bf16[128,1024]{1,0:T(8,128)(2,1)S(1)}, bf16[128,1024]{1,0:T(8,128)(2,1)S(1)}, u32[]{:S(2)}, u32[]{:S(2)}) collective-permute-start(bf16[128,1024]{1,0:T(8,128)(2,1)S(1)} %slice.213), channel_id=1, source_target_pairs={{0,16},{16,0},{1,17},{17,1},{2,18},{18,2},{3,19},{19,3},{4,20},{20... | collective-permute-start | bytes 786440 | tf_op jit(solution)/shard_map/ppermute | solution.py:57
  198.0 8.2 %collective-permute-start.12 = (bf16[128,1024]{1,0:T(8,128)(2,1)S(1)}, bf16[128,1024]{1,0:T(8,128)(2,1)S(1)}, u32[]{:S(2)}, u32[]{:S(2)}) collective-permute-start(bf16[128,1024]{1,0:T(8,128)(2,1)S(1)} %slice.214), channel_id=1, source_target_pairs={{0,2},{2,0},{1,3},{3,1},{4,6},{6,4},{5,7},{7,5},{8,10},{10,8},{9,1... | collective-permute-start | bytes 786440 | tf_op jit(solution)/shard_map/ppermute | solution.py:57
  224.4 8.2 %collective-permute-start.22 = (bf16[128,1024]{1,0:T(8,128)(2,1)S(1)}, bf16[128,1024]{1,0:T(8,128)(2,1)S(1)}, u32[]{:S(2)}, u32[]{:S(2)}) collective-permute-start(bf16[128,1024]{1,0:T(8,128)(2,1)S(1)} %get-tuple-element.189), channel_id=1, source_target_pairs={{0,16},{16,0},{1,17},{17,1},{2,18},{18,2},{3,19},{19,3},{4,20},{20... | collective-permute-start | bytes 786440 | tf_op jit(solution)/shard_map/ppermute | solution.py:57
  225.0 7.6 %collective-permute-start.24 = (bf16[128,1024]{1,0:T(8,128)(2,1)S(1)}, bf16[128,1024]{1,0:T(8,128)(2,1)S(1)}, u32[]{:S(2)}, u32[]{:S(2)}) collective-permute-start(bf16[128,1024]{1,0:T(8,128)(2,1)S(1)} %get-tuple-element.188), channel_id=1, source_target_pairs={{0,2},{2,0},{1,3},{3,1},{4,6},{6,4},{5,7},{7,5},{8,10},{10,8},{9,1... | collective-permute-start | bytes 786440 | tf_op jit(solution)/shard_map/ppermute | solution.py:57
  229.7 9.3 %collective-permute-start.14 = (bf16[128,1024]{1,0:T(8,128)(2,1)S(1)}, bf16[128,1024]{1,0:T(8,128)(2,1)S(1)}, u32[]{:S(2)}, u32[]{:S(2)}) collective-permute-start(bf16[128,1024]{1,0:T(8,128)(2,1)S(1)} %get-tuple-element.195), channel_id=1, source_target_pairs={{0,16},{16,0},{1,17},{17,1},{2,18},{18,2},{3,19},{19,3},{4,20},{20... | collective-permute-start | bytes 786440 | tf_op jit(solution)/shard_map/ppermute | solution.py:57
  231.2 9.2 %collective-permute-start.16 = (bf16[128,1024]{1,0:T(8,128)(2,1)S(1)}, bf16[128,1024]{1,0:T(8,128)(2,1)S(1)}, u32[]{:S(2)}, u32[]{:S(2)}) collective-permute-start(bf16[128,1024]{1,0:T(8,128)(2,1)S(1)} %get-tuple-element.194), channel_id=1, source_target_pairs={{0,2},{2,0},{1,3},{3,1},{4,6},{6,4},{5,7},{7,5},{8,10},{10,8},{9,1... | collective-permute-start | bytes 786440 | tf_op jit(solution)/shard_map/ppermute | solution.py:57
  232.8 18.9 %collective-permute-start.23 = (bf16[256,1024]{1,0:T(8,128)(2,1)S(1)}, bf16[256,1024]{1,0:T(8,128)(2,1)S(1)}, u32[]{:S(2)}, u32[]{:S(2)}) collective-permute-start(bf16[256,1024]{1,0:T(8,128)(2,1)S(1)} %pad_maximum_fusion.10), channel_id=1, source_target_pairs={{0,2},{2,0},{1,3},{3,1},{4,6},{6,4},{5,7},{7,5},{8,10},{10,8},{9,1... | collective-permute-start | bytes 1572872 | tf_op jit(solution)/shard_map/ppermute | solution.py:57
  235.3 16.4 %collective-permute-start.25 = (bf16[256,1024]{1,0:T(8,128)(2,1)S(1)}, bf16[256,1024]{1,0:T(8,128)(2,1)S(1)}, u32[]{:S(2)}, u32[]{:S(2)}) collective-permute-start(bf16[256,1024]{1,0:T(8,128)(2,1)S(1)} %pad_maximum_fusion.11), channel_id=1, source_target_pairs={{0,16},{16,0},{1,17},{17,1},{2,18},{18,2},{3,19},{19,3},{4,20},{20... | collective-permute-start | bytes 1572872 | tf_op jit(solution)/shard_map/ppermute | solution.py:57
  240.7 19.5 %collective-permute-start.15 = (bf16[256,1024]{1,0:T(8,128)(2,1)S(1)}, bf16[256,1024]{1,0:T(8,128)(2,1)S(1)}, u32[]{:S(2)}, u32[]{:S(2)}) collective-permute-start(bf16[256,1024]{1,0:T(8,128)(2,1)S(1)} %pad_maximum_fusion.8), channel_id=1, source_target_pairs={{0,2},{2,0},{1,3},{3,1},{4,6},{6,4},{5,7},{7,5},{8,10},{10,8},{9,1... | collective-permute-start | bytes 1572872 | tf_op jit(solution)/shard_map/ppermute | solution.py:57
  241.4 18.8 %collective-permute-start.17 = (bf16[256,1024]{1,0:T(8,128)(2,1)S(1)}, bf16[256,1024]{1,0:T(8,128)(2,1)S(1)}, u32[]{:S(2)}, u32[]{:S(2)}) collective-permute-start(bf16[256,1024]{1,0:T(8,128)(2,1)S(1)} %pad_maximum_fusion.9), channel_id=1, source_target_pairs={{0,16},{16,0},{1,17},{17,1},{2,18},{18,2},{3,19},{19,3},{4,20},{20... | collective-permute-start | bytes 1572872 | tf_op jit(solution)/shard_map/ppermute | solution.py:57
  263.1 12.0 %collective-permute-start.26 = (bf16[256,1024]{1,0:T(8,128)(2,1)S(1)}, bf16[256,1024]{1,0:T(8,128)(2,1)S(1)}, u32[]{:S(2)}, u32[]{:S(2)}) collective-permute-start(bf16[256,1024]{1,0:T(8,128)(2,1)S(1)} %get-tuple-element.171), channel_id=1, source_target_pairs={{0,2},{2,0},{1,3},{3,1},{4,6},{6,4},{5,7},{7,5},{8,10},{10,8},{9,1... | collective-permute-start | bytes 1572872 | tf_op jit(solution)/shard_map/ppermute | solution.py:57
  264.6 12.9 %collective-permute-start.27 = (bf16[256,1024]{1,0:T(8,128)(2,1)S(1)}, bf16[256,1024]{1,0:T(8,128)(2,1)S(1)}, u32[]{:S(2)}, u32[]{:S(2)}) collective-permute-start(bf16[256,1024]{1,0:T(8,128)(2,1)S(1)} %get-tuple-element.171), channel_id=1, source_target_pairs={{0,16},{16,0},{1,17},{17,1},{2,18},{18,2},{3,19},{19,3},{4,20},{20... | collective-permute-start | bytes 1572872 | tf_op jit(solution)/shard_map/ppermute | solution.py:57
  275.2 6.8 %collective-permute-start.28 = (bf16[128,1024]{1,0:T(8,128)(2,1)S(1)}, bf16[128,1024]{1,0:T(8,128)(2,1)S(1)}, u32[]{:S(2)}, u32[]{:S(2)}) collective-permute-start(bf16[128,1024]{1,0:T(8,128)(2,1)S(1)} %slice.233), channel_id=1, source_target_pairs={{0,16},{16,0},{1,17},{17,1},{2,18},{18,2},{3,19},{19,3},{4,20},{20... | collective-permute-start | bytes 786440 | tf_op jit(solution)/shard_map/ppermute | solution.py:57
  287.1 66.0 %reduce-scatter.14.cloned.1.call-start = ((), (), s32[]{:S(2)}) async-start(), calls=%async_computation.14 | async-start | bytes 2654208 | tf_op jit(solution)/shard_map/reduce_scatter | solution.py:656
  293.5 114.1 %reduce-scatter.6.cloned.1.call-start = ((), (), s32[]{:S(2)}) async-start(), calls=%async_computation.10 | async-start | bytes 4718592 | tf_op jit(solution)/shard_map/reduce_scatter | solution.py:677
  318.4 148.5 %reduce-scatter.12.cloned.1.call-start = ((), (), s32[]{:S(2)}) async-start(), calls=%async_computation.13 | async-start | bytes 5308416 | tf_op jit(solution)/shard_map/reduce_scatter | solution.py:138
  335.4 84.3 %collective-permute-start.39 = (bf16[32,1024]{1,0:T(8,128)(2,1)}, bf16[32,1024]{1,0:T(8,128)(2,1)S(1)}, u32[]{:S(2)}, u32[]{:S(2)}) collective-permute-start(bf16[32,1024]{1,0:T(8,128)(2,1)} %reduce-scatter.10.cloned.1.call-done), channel_id=1, source_target_pairs={{0,0},{1,1},{4,2},{5,3},{8,4},{9,5},{12,6},{13,7},{2,8},{3,9},{6,1... | collective-permute-start | bytes 196616 | tf_op jit(solution)/shard_map/ppermute | solution.py:163
  353.1 67.3 %collective-permute-start.40 = (bf16[144,1024]{1,0:T(8,128)(2,1)}, bf16[144,1024]{1,0:T(8,128)(2,1)}, u32[]{:S(2)}, u32[]{:S(2)}) collective-permute-start(bf16[144,1024]{1,0:T(8,128)(2,1)} %reduce-scatter.14.cloned.1.call-done), channel_id=1, source_target_pairs={{0,0},{1,1},{4,2},{5,3},{8,4},{9,5},{12,6},{13,7},{2,8},{3,9},{6,1... | collective-permute-start | bytes 884744 | tf_op jit(solution)/shard_map/ppermute | solution.py:163
  419.7 51.1 %collective-permute-start.34 = (f32[2176]{0:T(1024)S(1)}, f32[2176]{0:T(1024)S(1)}, u32[]{:S(2)}, u32[]{:S(2)}) collective-permute-start(f32[2176]{0:T(1024)S(1)} %concatenate.95), channel_id=1, source_target_pairs={{0,1},{1,0},{2,3},{3,2},{4,5},{5,4},{6,7},{7,6},{8,9},{9,8},{10,11... | collective-permute-start | bytes 26120 | tf_op jit(solution)/shard_map/ppermute | solution.py:109
  466.9 16.4 %all-to-all-start.3 = ((bf16[4,32,2304]{2,1,0:T(8,128)(2,1)}), bf16[4,32,2304]{2,1,0:T(8,128)(2,1)S(1)}, u32[]{:S(2)}, u32[]{:S(2)}) async-start(bf16[4,32,2304]{2,1,0:T(8,128)(2,1)} %bitcast.298), calls=%async_computation.7 | async-start | bytes 1179648 | tf_op jit(solution)/shard_map/all_to_all | solution.py:115
  470.6 36.2 %reduce-scatter.8.cloned.1.call-start = ((), (), s32[]{:S(2)}) async-start(), calls=%async_computation.11 | async-start | bytes 1179648 | tf_op jit(solution)/shard_map/reduce_scatter | solution.py:138
  470.8 6.9 %collective-permute-start.35 = (f32[2176]{0:T(1024)S(1)}, f32[2176]{0:T(1024)S(1)}, u32[]{:S(2)}, u32[]{:S(2)}) collective-permute-start(f32[2176]{0:T(1024)S(1)} %add.351), channel_id=1, source_target_pairs={{0,2},{2,0},{1,3},{3,1},{4,6},{6,4},{5,7},{7,5},{8,10},{10,8},{9,1... | collective-permute-start | bytes 26120 | tf_op jit(solution)/shard_map/ppermute | solution.py:109
  480.0 7.8 %collective-permute-start.30 = (bf16[128,1024]{1,0:T(8,128)(2,1)}, bf16[128,1024]{1,0:T(8,128)(2,1)S(1)}, u32[]{:S(2)}, u32[]{:S(2)}) collective-permute-start(bf16[128,1024]{1,0:T(8,128)(2,1)} %get-tuple-element.183), channel_id=1, source_target_pairs={{0,16},{16,0},{1,17},{17,1},{2,18},{18,2},{3,19},{19,3},{4,20},{20... | collective-permute-start | bytes 786440 | tf_op jit(solution)/shard_map/ppermute | solution.py:57
  480.6 7.3 %collective-permute-start.32 = (bf16[128,1024]{1,0:T(8,128)(2,1)}, bf16[128,1024]{1,0:T(8,128)(2,1)S(1)}, u32[]{:S(2)}, u32[]{:S(2)}) collective-permute-start(bf16[128,1024]{1,0:T(8,128)(2,1)} %get-tuple-element.182), channel_id=1, source_target_pairs={{0,2},{2,0},{1,3},{3,1},{4,6},{6,4},{5,7},{7,5},{8,10},{10,8},{9,1... | collective-permute-start | bytes 786440 | tf_op jit(solution)/shard_map/ppermute | solution.py:57
  485.5 8.4 %collective-permute-start.38 = (f32[2176]{0:T(1024)S(1)}, f32[2176]{0:T(1024)S(1)}, u32[]{:S(2)}, u32[]{:S(2)}) collective-permute-start(f32[2176]{0:T(1024)S(1)} %add.354), channel_id=1, source_target_pairs={{0,8},{4,12},{8,0},{12,4},{1,9},{5,13},{9,1},{13,5},{2,10},{6,14},... | collective-permute-start | bytes 26120 | tf_op jit(solution)/shard_map/ppermute | solution.py:109
  489.1 11.2 %collective-permute-start.31 = (bf16[256,1024]{1,0:T(8,128)(2,1)S(1)}, bf16[256,1024]{1,0:T(8,128)(2,1)S(1)}, u32[]{:S(2)}, u32[]{:S(2)}) collective-permute-start(bf16[256,1024]{1,0:T(8,128)(2,1)S(1)} %pad_maximum_fusion.12), channel_id=1, source_target_pairs={{0,2},{2,0},{1,3},{3,1},{4,6},{6,4},{5,7},{7,5},{8,10},{10,8},{9,1... | collective-permute-start | bytes 1572872 | tf_op jit(solution)/shard_map/ppermute | solution.py:57
  490.5 11.1 %collective-permute-start.33 = (bf16[256,1024]{1,0:T(8,128)(2,1)S(1)}, bf16[256,1024]{1,0:T(8,128)(2,1)S(1)}, u32[]{:S(2)}, u32[]{:S(2)}) collective-permute-start(bf16[256,1024]{1,0:T(8,128)(2,1)S(1)} %pad_maximum_fusion.13), channel_id=1, source_target_pairs={{0,16},{16,0},{1,17},{17,1},{2,18},{18,2},{3,19},{19,3},{4,20},{20... | collective-permute-start | bytes 1572872 | tf_op jit(solution)/shard_map/ppermute | solution.py:57
  506.8 8.7 %all-to-all-start.2 = ((bf16[4,32,512]{2,1,0:T(8,128)(2,1)}), bf16[4,32,512]{2,1,0:T(8,128)(2,1)S(1)}, u32[]{:S(2)}, u32[]{:S(2)}) async-start(bf16[4,32,512]{2,1,0:T(8,128)(2,1)} %bitcast.302), calls=%async_computation.4 | async-start | bytes 262144 | tf_op jit(solution)/shard_map/all_to_all | solution.py:115
  (53 other events, 459.4 us)
Sparse Core Ops, SparseCore 0:
  26.0 22.4 all-gather.10
  58.2 50.1 all-gather.8
  110.0 30.1 all-gather.14
  141.7 50.8 all-gather.12
  287.3 29.1 reduce-scatter.9
  318.7 34.3 reduce-scatter.13
  355.5 52.0 reduce-scatter.5
  410.0 56.8 reduce-scatter.11
  476.9 29.7 reduce-scatter.7
